TPU v7x, 32 devices: a whole 2x2x4 slice. The times are simulated.
32 devices in a mesh: dp: 2 (over core), mp: 16 (over z, y, x).
Axes of the slice: x: 2, y: 2, z: 4, core: 2. Of those that a mesh axis runs over, the one named last changes fastest.
Arguments:
- tokens: bfloat16 [8192, 1024], P(('dp', 'mp')), may hold values from -6 to 6
- cotangent: bfloat16 [8192, 1024], P(('dp', 'mp')), may hold values from -6 to 6
- seq_lengths: int32 [2, 4], P('dp'), may hold values from 1 to 2048, 4096 in all within a row
- first_gain: float32 [1024], replicated, may hold values from 0.1 to 1.9
- first_bias: float32 [1024], replicated, may hold values from -2 to 2
- second_gain: float32 [1024], replicated, may hold values from 0.1 to 1.9
- second_bias: float32 [1024], replicated, may hold values from -2 to 2
- blend_key: float32 [1024], replicated, may hold values from 0 to 1
- blend_value: float32 [1024], replicated, may hold values from 0 to 1
- blend_recept: float32 [1024], replicated, may hold values from 0 to 1
- channel_key: float32 [1024], replicated, may hold values from 0 to 1
- channel_recept: float32 [1024], replicated, may hold values from 0 to 1
- time_decay: float32 [1024], P('mp'), may hold values from -8 to -2
- time_first: float32 [1024], P('mp'), may hold values from -1 to 1
- weight_key: bfloat16 [1024, 1024], P(None, 'mp'), may hold values from -0.1875 to 0.1875
- weight_value: bfloat16 [1024, 1024], P(None, 'mp'), may hold values from -0.1875 to 0.1875
- weight_recept: bfloat16 [1024, 1024], P(None, 'mp'), may hold values from -0.1875 to 0.1875
- weight_output: bfloat16 [1024, 1024], P('mp'), may hold values from -0.75 to 0.75
- hidden_key: bfloat16 [1024, 4096], P(None, 'mp'), may hold values from -0.1875 to 0.1875
- hidden_value: bfloat16 [4096, 1024], P('mp'), may hold values from -0.09375 to 0.09375
- hidden_recept: bfloat16 [1024, 1024], P(None, 'mp'), may hold values from -0.1875 to 0.1875
Outputs:
- block_out: bfloat16 [8192, 1024], P(('dp', 'mp'))
- grad_tokens: float32 [8192, 1024], P(('dp', 'mp'))
- grad_first_gain: float32 [1024], replicated
- grad_first_bias: float32 [1024], replicated
- grad_second_gain: float32 [1024], replicated
- grad_second_bias: float32 [1024], replicated
- grad_blend_key: float32 [1024], replicated
- grad_blend_value: float32 [1024], replicated
- grad_blend_recept: float32 [1024], replicated
- grad_channel_key: float32 [1024], replicated
- grad_channel_recept: float32 [1024], replicated
- grad_time_decay: float32 [1024], P('mp')
- grad_time_first: float32 [1024], P('mp')
- grad_weight_key: float32 [1024, 1024], P(None, 'mp')
- grad_weight_value: float32 [1024, 1024], P(None, 'mp')
- grad_weight_recept: float32 [1024, 1024], P(None, 'mp')
- grad_weight_output: float32 [1024, 1024], P('mp')
- grad_hidden_key: float32 [1024, 4096], P(None, 'mp')
- grad_hidden_value: float32 [4096, 1024], P('mp')
- grad_hidden_recept: float32 [1024, 1024], P(None, 'mp')
Inputs may be any that keep to these rules, and one draw needn't show every extreme that they name: `seq_lengths`: each row sums to 4096; its largest entry is exactly 2048.
All inputs are finite; a program needn't handle non-finite values.
Results may differ from a plain program's by a relative error of at most 0.03.
Values may be sent and summed in bfloat16 or wider, within the bound.
No kernel may reach another device: no remote copies, remote signals or barrier semaphores. Data moves between devices by JAX's collectives and lax.ppermute only.
A program may use at most 576 MiB of HBM per device.

v0:
```python
import math

import jax
import jax.numpy as jnp
from jax import lax
from jax.sharding import PartitionSpec as P

norm_eps = 1e-05
highest = lax.Precision.HIGHEST


def layer_norm(source, norm_gain, norm_bias):
    centre = jnp.mean(source, axis=-1, keepdims=True)
    spread = source - centre
    scaled = spread * lax.rsqrt(jnp.mean(spread * spread, axis=-1, keepdims=True) + norm_eps)
    return scaled * norm_gain + norm_bias


def shifted_down(source, head_row, keep_flag):
    moved = jnp.concatenate([head_row, source[:-1]], axis=0)
    return moved.astype(jnp.float32) * keep_flag


def blend_pair(present_memory, before, factor):
    return present_memory.astype(jnp.float32) * factor + before * (1.0 - factor)


def outer_sum(left, right):
    return lax.dot_general(
        left, right, (((0,), (0,)), ((), ())), preferred_element_type=jnp.float32
    )


def against(left, weight):
    return lax.dot_general(
        left, weight, (((1,), (1,)), ((), ())), preferred_element_type=jnp.float32
    )


def blend_back(present_memory, before, keep_flag, grads, factors, tail_row):
    direct = grads[0] * factors[0]
    spill = grads[0] * (1.0 - factors[0])
    for grad_part, factor in zip(grads[1:], factors[1:]):
        direct = direct + grad_part * factor
        spill = spill + grad_part * (1.0 - factor)
    spill = spill * keep_flag
    passed = jnp.concatenate([spill[1:], tail_row], axis=0)
    change = present_memory.astype(jnp.float32) - before
    totals = [jnp.sum(grad_part * change, axis=0) for grad_part in grads]
    return (direct + passed, totals)


def sequence_starts(lengths, count_rows):
    places = jnp.arange(count_rows, dtype=jnp.int32)
    ends = jnp.cumsum(lengths)
    opening_markers = jnp.sum(
        jnp.where(ends[None, :] <= places[:, None], lengths[None, :], 0), axis=1
    )
    return (opening_markers, places)


def scaled_payload_here(
    lookup_lines, payload_table, fading_speed, reward_coefficient, opening_markers
):
    length_all, channels = lookup_lines.shape
    block_len = math.gcd(length_all, 128)
    blocks = length_all // block_len
    rate = jnp.exp(fading_speed)[:, None, None]
    lookup_fields = lookup_lines.T.reshape(channels, blocks, block_len)
    value_cols = payload_table.T.reshape(channels, blocks, block_len)
    place = jnp.arange(block_len, dtype=jnp.float32)
    index = jnp.arange(length_all, dtype=jnp.int32).reshape(blocks, block_len)
    start_blk = opening_markers.reshape(blocks, block_len)
    growth = jnp.exp(lookup_fields + rate * place)
    falling = jnp.exp(-rate * (place - 1.0))
    lower = jnp.arange(block_len)[None, :] < jnp.arange(block_len)[:, None]
    inside = (lower[None] & (index[:, None, :] >= start_blk[:, :, None])).astype(jnp.float32)
    weighted = growth * value_cols
    numer = jnp.einsum("nti,cni->cnt", inside, weighted, precision=highest) * falling
    denom = jnp.einsum("nti,cni->cnt", inside, growth, precision=highest) * falling
    last_start = start_blk[:, -1]
    tail_mask = (index >= last_start[:, None]).astype(jnp.float32)[None]
    end_fall = jnp.exp(-rate[:, :, 0] * (block_len - 1.0))
    end_num = jnp.sum(tail_mask * weighted, axis=2) * end_fall
    end_den = jnp.sum(tail_mask * growth, axis=2) * end_fall
    carry_on = (last_start < index[:, 0]).astype(jnp.float32)
    pass_factor = jnp.exp(-rate[:, :, 0] * block_len) * carry_on[None, :]

    def combine(early, late):
        return (early[0] * late[0], late[0] * early[1] + late[1], late[0] * early[2] + late[2])

    _, run_num, run_den = lax.associative_scan(combine, (pass_factor, end_num, end_den), axis=1)
    state_num = jnp.concatenate([jnp.zeros_like(run_num[:, :1]), run_num[:, :-1]], axis=1)
    state_den = jnp.concatenate([jnp.zeros_like(run_den[:, :1]), run_den[:, :-1]], axis=1)
    reach = (start_blk < index[:, :1]).astype(jnp.float32)[None]
    fading_argument = jnp.exp(-rate * place) * reach
    numer = numer + state_num[:, :, None] * fading_argument
    denom = denom + state_den[:, :, None] * fading_argument
    present_memory = jnp.exp(reward_coefficient[:, None, None] + lookup_fields)
    result = (numer + present_memory * value_cols) / (denom + present_memory)
    return result.reshape(channels, length_all).T


def small_table(first_pair, mixer_small, second_pair, ffn_small, shard_count):
    small_all = jnp.concatenate(list(first_pair) + mixer_small + list(second_pair) + ffn_small)
    return jnp.broadcast_to(small_all[None, :], (shard_count, small_all.shape[0]))


def shards(
    tokens,
    cotangent,
    seq_lengths,
    first_gain,
    first_bias,
    second_gain,
    second_bias,
    blend_key,
    blend_value,
    blend_recept,
    channel_key,
    channel_recept,
    time_decay,
    time_first,
    weight_key,
    weight_value,
    weight_recept,
    weight_output,
    hidden_key,
    hidden_value,
    hidden_recept,
):
    shard_count = lax.axis_size("mp")
    local_rows = tokens.shape[0]
    width = tokens.shape[1]
    group_rows = local_rows * shard_count
    opening_markers, places = sequence_starts(seq_lengths[0], group_rows)
    keep_all = (places > opening_markers).astype(jnp.float32)[:, None]
    zero_row = jnp.zeros((1, width), jnp.bfloat16)
    zero_grad = jnp.zeros((1, width), jnp.float32)

    def scaled_payload_incomplete(
        lookup_argument, payload_argument, fading_argument, reward_argument
    ):
        return scaled_payload_here(
            lookup_argument, payload_argument, fading_argument, reward_argument, opening_markers
        )

    gathered = lax.all_gather(tokens, "mp", axis=0, tiled=True)
    normed_full, first_back = jax.vjp(
        layer_norm, gathered.astype(jnp.float32), first_gain, first_bias
    )
    normed = normed_full.astype(jnp.bfloat16)
    before = shifted_down(normed, zero_row, keep_all)
    mix_key_in = blend_pair(normed, before, blend_key).astype(jnp.bfloat16)
    mix_value_in = blend_pair(normed, before, blend_value).astype(jnp.bfloat16)
    mix_recept_in = blend_pair(normed, before, blend_recept).astype(jnp.bfloat16)
    lookup_lines = jnp.dot(mix_key_in, weight_key, preferred_element_type=jnp.float32)
    payload_table = jnp.dot(mix_value_in, weight_value, preferred_element_type=jnp.float32)
    recept = jnp.dot(mix_recept_in, weight_recept, preferred_element_type=jnp.float32)
    mixed, wkv_back = jax.vjp(
        scaled_payload_incomplete, lookup_lines, payload_table, time_decay, time_first
    )
    opened = jax.nn.sigmoid(recept)
    gated = (opened * mixed).astype(jnp.bfloat16)
    attended = lax.psum_scatter(
        jnp.dot(gated, weight_output, preferred_element_type=jnp.float32),
        "mp",
        scatter_dimension=0,
        tiled=True,
    )
    hidden_rows = tokens.astype(jnp.float32) + attended
    second_full, second_back = jax.vjp(layer_norm, hidden_rows, second_gain, second_bias)
    second_low = second_full.astype(jnp.bfloat16)
    grad_out = cotangent.astype(jnp.float32)
    wide_rows = lax.all_gather(second_low, "mp", axis=0, tiled=True)
    prior = shifted_down(wide_rows, zero_row, keep_all)
    lookup_argument = blend_pair(wide_rows, prior, channel_key).astype(jnp.bfloat16)
    recept_in = blend_pair(wide_rows, prior, channel_recept).astype(jnp.bfloat16)
    ffn_pre = jnp.dot(lookup_argument, hidden_key, preferred_element_type=jnp.float32)
    squared = jnp.square(jax.nn.relu(ffn_pre)).astype(jnp.bfloat16)
    carried = lax.psum_scatter(
        jnp.dot(squared, hidden_value, preferred_element_type=jnp.float32).astype(jnp.bfloat16),
        "mp",
        scatter_dimension=0,
        tiled=True,
    ).astype(jnp.float32)
    gate_cols = jax.nn.sigmoid(
        jnp.dot(recept_in, hidden_recept, preferred_element_type=jnp.float32)
    )
    ffn_gate = lax.all_to_all(gate_cols, "mp", split_axis=0, concat_axis=1, tiled=True)
    block_rows = hidden_rows + ffn_gate * carried
    grad_carried = (grad_out * ffn_gate).astype(jnp.bfloat16)
    grad_gate_pre = (grad_out * carried * ffn_gate * (1.0 - ffn_gate)).astype(jnp.bfloat16)
    grad_gate_cols = lax.all_to_all(grad_gate_pre, "mp", split_axis=1, concat_axis=0, tiled=True)
    grad_wide = lax.all_gather(grad_carried, "mp", axis=0, tiled=True)
    grad_hidden_value = outer_sum(squared, grad_wide)
    grad_pre = (against(grad_wide, hidden_value) * 2.0 * jax.nn.relu(ffn_pre)).astype(jnp.bfloat16)
    grad_hidden_key = outer_sum(lookup_argument, grad_pre)
    grad_hidden_recept = outer_sum(recept_in, grad_gate_cols)
    grad_key_two = against(grad_pre, hidden_key)
    grad_recept_two = against(grad_gate_cols, hidden_recept)
    grad_second_part, ffn_small = blend_back(
        wide_rows,
        prior,
        keep_all,
        (grad_key_two, grad_recept_two),
        (channel_key, channel_recept),
        zero_grad,
    )
    grad_second = lax.psum_scatter(
        grad_second_part.astype(jnp.bfloat16), "mp", scatter_dimension=0, tiled=True
    ).astype(jnp.float32)
    block_out = block_rows.astype(jnp.bfloat16)
    grad_from_norm, grad_second_gain, grad_second_bias = second_back(grad_second)
    grad_hidden = grad_out + grad_from_norm
    grad_attended = grad_hidden.astype(jnp.bfloat16)
    grad_att_all = lax.all_gather(grad_attended, "mp", axis=0, tiled=True)
    grad_weight_output = outer_sum(gated, grad_att_all)
    grad_gated = against(grad_att_all, weight_output)
    grad_mixed = grad_gated * opened
    grad_recept = (grad_gated * mixed * opened * (1.0 - opened)).astype(jnp.bfloat16)
    grad_keys_full, grad_values_full, grad_time_decay, grad_time_first = wkv_back(grad_mixed)
    grad_keys = grad_keys_full.astype(jnp.bfloat16)
    grad_values = grad_values_full.astype(jnp.bfloat16)
    grad_weight_key = outer_sum(mix_key_in, grad_keys)
    grad_weight_value = outer_sum(mix_value_in, grad_values)
    grad_weight_recept = outer_sum(mix_recept_in, grad_recept)
    grad_key_one = against(grad_keys, weight_key)
    grad_value_one = against(grad_values, weight_value)
    grad_recept_one = against(grad_recept, weight_recept)
    grad_normed, mixer_small = blend_back(
        normed,
        before,
        keep_all,
        (grad_key_one, grad_value_one, grad_recept_one),
        (blend_key, blend_value, blend_recept),
        zero_grad,
    )
    grad_raw, grad_first_gain, grad_first_bias = first_back(grad_normed)
    tiled = small_table(
        (grad_first_gain, grad_first_bias),
        mixer_small,
        (grad_second_gain, grad_second_bias),
        ffn_small,
        shard_count,
    )
    grad_rows, small_sum = (
        lax.psum_scatter(
            grad_raw.astype(jnp.bfloat16), "mp", scatter_dimension=0, tiled=True
        ).astype(jnp.float32),
        lax.psum_scatter(tiled.astype(jnp.bfloat16), "mp", scatter_dimension=0, tiled=True).astype(
            jnp.float32
        ),
    )
    grad_tokens = grad_hidden + grad_rows
    reduced = (
        lax.psum(grad_weight_key.astype(jnp.bfloat16), "dp").astype(jnp.float32),
        lax.psum(grad_weight_value.astype(jnp.bfloat16), "dp").astype(jnp.float32),
        lax.psum(grad_weight_recept.astype(jnp.bfloat16), "dp").astype(jnp.float32),
        lax.psum(grad_weight_output.astype(jnp.bfloat16), "dp").astype(jnp.float32),
        lax.psum(grad_hidden_key.astype(jnp.bfloat16), "dp").astype(jnp.float32),
        lax.psum(grad_hidden_value.astype(jnp.bfloat16), "dp").astype(jnp.float32),
        lax.psum(grad_hidden_recept.astype(jnp.bfloat16), "dp").astype(jnp.float32),
        lax.psum(grad_time_decay.astype(jnp.bfloat16), "dp").astype(jnp.float32),
        lax.psum(grad_time_first.astype(jnp.bfloat16), "dp").astype(jnp.float32),
        lax.psum(small_sum[0].astype(jnp.bfloat16), "dp").astype(jnp.float32),
    )
    small_parts = reduced[9].reshape(9, width)
    return (
        block_out,
        grad_tokens,
        small_parts[0],
        small_parts[1],
        small_parts[5],
        small_parts[6],
        small_parts[2],
        small_parts[3],
        small_parts[4],
        small_parts[7],
        small_parts[8],
        reduced[7],
        reduced[8],
        reduced[0],
        reduced[1],
        reduced[2],
        reduced[3],
        reduced[4],
        reduced[5],
        reduced[6],
    )


def solution(mesh):
    placed = (
        P(("dp", "mp"), None),
        P(("dp", "mp"), None),
        P("dp", None),
        P(),
        P(),
        P(),
        P(),
        P(),
        P(),
        P(),
        P(),
        P(),
        P("mp"),
        P("mp"),
        P(None, "mp"),
        P(None, "mp"),
        P(None, "mp"),
        P("mp", None),
        P(None, "mp"),
        P("mp", None),
        P(None, "mp"),
    )
    return jax.shard_map(
        shards,
        mesh=mesh,
        in_specs=placed,
        out_specs=(
            P(("dp", "mp"), None),
            P(("dp", "mp"), None),
            P(),
            P(),
            P(),
            P(),
            P(),
            P(),
            P(),
            P(),
            P(),
            P("mp"),
            P("mp"),
            P(None, "mp"),
            P(None, "mp"),
            P(None, "mp"),
            P("mp", None),
            P(None, "mp"),
            P("mp", None),
            P(None, "mp"),
        ),
        check_vma=False,
    )
```

profile of v0, /device:TPU:1, one launch (start us, length us, event | category | flops | bytes accessed | tf_op | source)
XLA Modules:
  0.0 1806.6 jit_solution(15917737168596817380)
XLA Ops:
  12.4 112.6 %all-gather.5.cloned.1.call-done = bf16[4096,1024]{1,0:T(8,128)(2,1)} async-done(((bf16[256,1024]{1,0:T(8,128)(2,1)}), bf16[4096,1024]{1,0:T(8,128)(2,1)}) %all-gather.5.cloned.1.call-update) | async-done | bytes 8388624 | tf_op jit(solution)/shard_map/all_gather | solution.py:148
  125.0 4.7 convert_reduce_fusion
  129.7 5.8 fusion.9
  135.6 5.2 fusion.7
  140.9 16.6 fusion.20
  157.5 3.3 copy-done.2
  160.8 2.7 convolution_bitcast_fusion.1
  163.5 6.1 convolution_bitcast_fusion
  171.6 3.2 fusion.38
  174.9 3.2 fusion.39
  179.4 3.2 divide_bitcast_fusion
  183.6 7.1 fusion.64
  191.5 8.2 fusion.152
  199.8 345.5 %reduce-scatter.5.cloned.1.call-done = f32[256,1024]{1,0:T(8,128)} async-done(((f32[4096,1024]{1,0:T(8,128)}), f32[256,1024]{1,0:T(8,128)}) %reduce-scatter.5.cloned.1.call-update) | async-done | bytes 1048592 | tf_op jit(solution)/shard_map/reduce_scatter | solution.py:165
  550.2 116.5 %all-gather.7.cloned.1.call-done = bf16[4096,1024]{1,0:T(8,128)(2,1)} async-done(((bf16[256,1024]{1,0:T(8,128)(2,1)}), bf16[4096,1024]{1,0:T(8,128)(2,1)}) %all-gather.7.cloned.1.call-update) | async-done | bytes 8388624 | tf_op jit(solution)/shard_map/all_gather | solution.py:175
  666.6 14.5 fusion.14
  681.2 3.4 copy-done.7
  684.6 2.4 convolution_maximum_fusion
  687.0 2.0 copy-done.3
  689.0 5.7 convolution_convert_fusion
  694.8 10.2 all-gather.9.cloned.1.call-start
  704.9 6.1 fusion.30
  711.1 36.1 %all_to_all.38 = f32[16,256,64]{1,2,0:T(8,128)} all-to-all(f32[16,256,64]{1,2,0:T(8,128)S(1)} %bitcast.221), channel_id=1, replica_groups=mesh['dp'=2,'mp'=16] {'mp'}, dimensions={0} | all-to-all | bytes 2097152 | tf_op jit(solution)/shard_map/all_to_all | solution.py:190
  747.2 2.5 copy.159
  749.7 133.1 %reduce-scatter.7.cloned.1.call-done = bf16[256,1024]{1,0:T(8,128)(2,1)} async-done(((bf16[4096,1024]{1,0:T(8,128)(2,1)}), bf16[256,1024]{1,0:T(8,128)(2,1)}) %reduce-scatter.7.cloned.1.call-update) | async-done | bytes 524304 | tf_op jit(solution)/shard_map/reduce_scatter | solution.py:181
  882.9 3.0 fusion.52
  885.9 2.1 copy.163
  888.0 7.7 all-to-all-start.1
  896.4 16.2 all-to-all-done.1
  914.5 9.1 fusion.154
  923.6 85.7 %all-gather.9.cloned.1.call-done = bf16[4096,1024]{1,0:T(8,128)(2,1)} async-done(((bf16[256,1024]{1,0:T(8,128)(2,1)}), bf16[4096,1024]{1,0:T(8,128)(2,1)}) %all-gather.9.cloned.1.call-update) | async-done | bytes 8388624 | tf_op jit(solution)/shard_map/all_gather | solution.py:195
  1009.3 7.2 fusion.27
  1016.5 8.9 fusion.153
  1025.5 13.0 fusion.25
  1038.5 15.3 add_convert_fusion.1
  1053.9 176.7 %reduce-scatter.9.cloned.1.call-done = bf16[256,1024]{1,0:T(8,128)(2,1)} async-done(((bf16[4096,1024]{1,0:T(8,128)(2,1)}), bf16[256,1024]{1,0:T(8,128)(2,1)}) %reduce-scatter.9.cloned.1.call-update) | async-done | bytes 524304 | tf_op jit(solution)/shard_map/reduce_scatter | solution.py:210
  1230.6 2.1 fusion.51
  1237.2 5.8 convolution_convert_fusion.3
  1243.0 6.7 convolution_convert_fusion.1
  1250.1 3.2 convolution_convert_fusion.2
  1253.9 97.8 %all-gather.11.cloned.1.call-done = bf16[4096,1024]{1,0:T(8,128)(2,1)} async-done(((bf16[256,1024]{1,0:T(8,128)(2,1)}), bf16[4096,1024]{1,0:T(8,128)(2,1)}) %all-gather.11.cloned.1.call-update) | async-done | bytes 8388624 | tf_op jit(solution)/shard_map/all_gather | solution.py:217
  1351.7 6.7 multiply_bitcast_fusion
  1358.5 3.7 fusion.122
  1363.1 3.6 multiply_reduce_fusion.7
  1371.7 3.5 fusion.45
  1376.8 5.8 convolution_convert_fusion.5
  1382.6 8.2 fusion.94
  1390.8 2.3 fusion.134
  1393.1 2.2 convolution_convert_fusion.6
  1395.3 8.1 fusion.97
  1403.4 2.2 convolution_convert_fusion.4
  1405.7 8.3 fusion.155
  1414.1 24.2 %fusion.22 = f32[4095,1024]{1,0:T(8,128)} fusion(f32[4096,1024]{1,0:T(8,128)} %fusion.155, f32[4096,1024]{1,0:T(8,128)} %fusion.94, f32[4096,1024]{1,0:T(8,128)} %fusion.97, f32[1024]{0:T(1024)S(1)} %copy-done.85, f32[1024]{0:T(1024)S(1)} %copy-done.93, f32[1024]{0:T(1024)S(1)} %copy-done.95, f32[4095]{0:T(1024)S(1)} %copy-done.38), kind=kLoop, calls=%fused_computation.33 | loop fusion | flops 25159680 | bytes 67121152 | tf_op jit(solution)/shard_map/mul | solution.py:46
  1438.5 45.9 %multiply_reduce_fusion = (bf16[1024]{0:T(1024)(128)(2,1)S(1)}, bf16[1024]{0:T(1024)(128)(2,1)S(1)}, bf16[1024]{0:T(1024)(128)(2,1)S(1)}, bf16[1024]{0:T(1024)(1...) fusion(f32[4096,1024]{1,0:T(8,128)} %fusion.154, ...), kind=kLoop, calls=%fused_computation.41 | loop fusion | flops 150983680 | bytes 151087104 | tf_op jit(solution)/shard_map/reduce_sum | solution.py:49
  1485.3 5.6 convolution_convert_fusion.7
  1491.0 10.3 fusion.129
  1501.5 4.0 add_convert_fusion
  1506.9 83.0 %all-reduce.91.cloned.1.call-done = bf16[16,9216]{1,0:T(8,128)(2,1)} async-done(((bf16[16,9216]{1,0:T(8,128)(2,1)}), bf16[16,9216]{1,0:T(8,128)(2,1)}) %all-reduce.91.cloned.1.call-update) | async-done | bytes 294928
  1591.6 5.7 all-reduce.86
  1598.9 17.8 all-reduce.93.cloned.1.call-done
  1624.8 2.1 convert_element_type.247
  1626.9 2.1 convert_element_type.249
  1629.1 168.3 %reduce-scatter.11.cloned.1.call-done = bf16[256,1024]{1,0:T(8,128)(2,1)} async-done(((bf16[4096,1024]{1,0:T(8,128)(2,1)}), bf16[256,1024]{1,0:T(8,128)(2,1)}) %reduce-scatter.11.cloned.1.call-update) | async-done | bytes 524304 | tf_op jit(solution)/shard_map/reduce_scatter | solution.py:248
  1797.3 2.3 convert_add_fusion.1
  (619 shorter events, 43.6 us)
Async XLA Ops:
  7.2 681.9 %copy-start = (bf16[256,1024]{1,0:T(8,128)(2,1)S(1)}, bf16[256,1024]{1,0:T(8,128)(2,1)}, u32[]{:S(2)}) copy-start(bf16[256,1024]{1,0:T(8,128)(2,1)} %param.40) | copy-start | bytes 1572868
  7.2 128.4 %copy-start.80 = (f32[1024]{0:T(1024)S(1)}, f32[1024]{0:T(1024)}, u32[]{:S(2)}) copy-start(f32[1024]{0:T(1024)} %param.24) | copy-start | bytes 12292
  7.2 128.4 %copy-start.106 = (f32[1024]{0:T(1024)S(1)}, f32[1024]{0:T(1024)}, u32[]{:S(2)}) copy-start(f32[1024]{0:T(1024)} %param.25) | copy-start | bytes 12292
  7.2 117.8 %all-gather.5.cloned.1.call-start = ((), (), s32[]{:S(2)}) async-start(), calls=%async_computation.6 | async-start | bytes 8912896 | tf_op jit(solution)/shard_map/all_gather | solution.py:148
  8.0 537.4 %reduce-scatter.5.cloned.1.call-start = ((), (), s32[]{:S(2)}) async-start(), calls=%async_computation.7 | async-start | bytes 17825792 | tf_op jit(solution)/shard_map/reduce_scatter | solution.py:165
  10.5 159.8 %copy-start.151 = (f32[64]{0:T(128)}, f32[64]{0:T(128)S(1)}, u32[]{:S(2)}) copy-start(f32[64]{0:T(128)S(1)} %get-tuple-element.190) | copy-start | bytes 772
  10.6 159.8 %copy-start.56 = (f32[64,16]{0,1:T(8,128)}, f32[64,16]{0,1:T(8,128)S(1)}, u32[]{:S(2)}) copy-start(f32[64,16]{0,1:T(8,128)S(1)} %slice.319) | copy-start | bytes 12292
  10.6 159.8 %copy-start.66 = (f32[64,16]{0,1:T(8,128)}, f32[64,16]{0,1:T(8,128)S(1)}, u32[]{:S(2)}) copy-start(f32[64,16]{0,1:T(8,128)S(1)} %slice.323) | copy-start | bytes 12292
  10.6 168.5 %copy-start.72 = (f32[64,15]{0,1:T(8,128)}, f32[64,15]{0,1:T(8,128)S(1)}, u32[]{:S(2)}) copy-start(f32[64,15]{0,1:T(8,128)S(1)} %slice.318) | copy-start | bytes 11524
  11.4 129.4 %copy-start.84 = (f32[1024]{0:T(1024)}, f32[1024]{0:T(1024)S(1)}, u32[]{:S(2)}) copy-start(f32[1024]{0:T(1024)S(1)} %broadcast_subtract_fusion.4) | copy-start | bytes 12292
  12.1 128.7 %copy-start.92 = (f32[1024]{0:T(1024)}, f32[1024]{0:T(1024)S(1)}, u32[]{:S(2)}) copy-start(f32[1024]{0:T(1024)S(1)} %get-tuple-element.194) | copy-start | bytes 12292
  12.1 128.7 %copy-start.94 = (f32[1024]{0:T(1024)}, f32[1024]{0:T(1024)S(1)}, u32[]{:S(2)}) copy-start(f32[1024]{0:T(1024)S(1)} %get-tuple-element.195) | copy-start | bytes 12292
  12.2 167.1 %copy-start.39 = (f32[32,128]{1,0:T(8,128)}, f32[32,128]{1,0:T(8,128)S(1)}, u32[]{:S(2)}) copy-start(f32[32,128]{1,0:T(8,128)S(1)} %compare_convert_fusion) | copy-start | bytes 49156
  12.3 167.0 %copy-start.35 = (f32[64,128]{1,0:T(8,128)}, f32[64,128]{1,0:T(8,128)S(1)}, u32[]{:S(2)}) copy-start(f32[64,128]{1,0:T(8,128)S(1)} %get-tuple-element.187) | copy-start | bytes 98308
  12.4 128.5 %copy-start.82 = (f32[1024]{0:T(1024)S(1)}, f32[1024]{0:T(1024)}, u32[]{:S(2)}) copy-start(f32[1024]{0:T(1024)} %param.30) | copy-start | bytes 12292
  12.4 128.5 %copy-start.88 = (f32[1024]{0:T(1024)S(1)}, f32[1024]{0:T(1024)}, u32[]{:S(2)}) copy-start(f32[1024]{0:T(1024)} %param.29) | copy-start | bytes 12292
  12.4 128.5 %copy-start.90 = (f32[1024]{0:T(1024)S(1)}, f32[1024]{0:T(1024)}, u32[]{:S(2)}) copy-start(f32[1024]{0:T(1024)} %param.28) | copy-start | bytes 12292
  191.5 353.8 %copy-start.23 = (bf16[256,1024]{1,0:T(8,128)(2,1)S(1)}, bf16[256,1024]{1,0:T(8,128)(2,1)}, u32[]{:S(2)}) copy-start(bf16[256,1024]{1,0:T(8,128)(2,1)} %param.21) | copy-start | bytes 1572868
  199.8 466.8 %all-gather.7.cloned.1.call-start = ((), (), s32[]{:S(2)}) async-start(), calls=%async_computation.8 | async-start | bytes 8912896 | tf_op jit(solution)/shard_map/all_gather | solution.py:175
  546.7 119.9 %copy-start.117 = (f32[256]{0:T(256)}, f32[256]{0:T(256)S(1)}, u32[]{:S(2)}) copy-start(f32[256]{0:T(256)S(1)} %broadcast_multiply_fusion.6) | copy-start | bytes 3076
  547.0 119.6 %copy-start.142 = (f32[256]{0:T(256)}, f32[256]{0:T(256)S(1)}, u32[]{:S(2)}) copy-start(f32[256]{0:T(256)S(1)} %multiply_reduce_fusion.8) | copy-start | bytes 3076
  547.0 119.6 %copy-start.126 = (f32[256]{0:T(256)}, f32[256]{0:T(256)S(1)}, u32[]{:S(2)}) copy-start(f32[256]{0:T(256)S(1)} %fusion.118) | copy-start | bytes 3076
  548.8 334.1 %reduce-scatter.7.cloned.1.call-start = ((), (), s32[]{:S(2)}) async-start(), calls=%async_computation.9 | async-start | bytes 8912896 | tf_op jit(solution)/shard_map/reduce_scatter | solution.py:181
  694.8 188.1 %copy-start.18 = (bf16[256,1024]{1,0:T(8,128)(2,1)S(1)}, bf16[256,1024]{1,0:T(8,128)(2,1)}, u32[]{:S(2)}) copy-start(bf16[256,1024]{1,0:T(8,128)(2,1)} %param.22) | copy-start | bytes 1572868
  694.8 314.5 %all-gather.9.cloned.1.call-start = ((), (), s32[]{:S(2)}) async-start(), calls=%async_computation.10 | async-start | bytes 8912896 | tf_op jit(solution)/shard_map/all_gather | solution.py:195
  888.0 24.6 %all-to-all-start.1 = ((bf16[256,16,64]{0,2,1:T(8,128)(2,1)}), bf16[256,16,64]{0,2,1:T(8,128)(2,1)S(1)}, u32[]{:S(2)}, u32[]{:S(2)}) async-start(bf16[256,16,64]{0,2,1:T(8,128)(2,1)} %bitcast.224), calls=%async_computation.3 | async-start | bytes 1048576 | tf_op jit(solution)/shard_map/all_to_all | solution.py:194
  895.7 334.9 %reduce-scatter.9.cloned.1.call-start = ((), (), s32[]{:S(2)}) async-start(), calls=%async_computation.11 | async-start | bytes 8912896 | tf_op jit(solution)/shard_map/reduce_scatter | solution.py:210
  1038.5 197.4 %copy-start.19 = (bf16[256,1024]{1,0:T(8,128)(2,1)S(1)}, bf16[256,1024]{1,0:T(8,128)(2,1)}, u32[]{:S(2)}) copy-start(bf16[256,1024]{1,0:T(8,128)(2,1)} %param.22) | copy-start | bytes 1572868
  1053.8 297.9 %all-gather.11.cloned.1.call-start = ((), (), s32[]{:S(2)}) async-start(), calls=%async_computation.12 | async-start | bytes 8912896 | tf_op jit(solution)/shard_map/all_gather | solution.py:217
  1236.9 353.0 %all-reduce.91.cloned.1.call-start = ((), (), s32[]{:S(2)}) async-start(), calls=%async_computation.14 | async-start | bytes 589824
  1249.7 117.0 %copy-start.59 = (f32[64,16]{0,1:T(8,128)S(1)}, f32[64,16]{0,1:T(8,128)}, u32[]{:S(2)}) copy-start(f32[64,16]{0,1:T(8,128)} %copy-done.58) | copy-start | bytes 12292
  1249.7 117.0 %copy-start.61 = (f32[64,16]{0,1:T(8,128)S(1)}, f32[64,16]{0,1:T(8,128)}, u32[]{:S(2)}) copy-start(f32[64,16]{0,1:T(8,128)} %copy-done.60) | copy-start | bytes 12292
  1249.8 117.8 %copy-start.75 = (f32[64,8]{0,1:T(8,128)S(1)}, f32[64,8]{0,1:T(8,128)}, u32[]{:S(2)}) copy-start(f32[64,8]{0,1:T(8,128)} %copy-done.74) | copy-start | bytes 6148
  1249.8 117.8 %copy-start.77 = (f32[64,8]{0,1:T(8,128)S(1)}, f32[64,8]{0,1:T(8,128)}, u32[]{:S(2)}) copy-start(f32[64,8]{0,1:T(8,128)} %copy-done.76) | copy-start | bytes 6148
  1249.8 117.8 %copy-start.105 = (f32[64,7]{0,1:T(8,128)S(1)}, f32[64,7]{0,1:T(8,128)}, u32[]{:S(2)}) copy-start(f32[64,7]{0,1:T(8,128)} %copy-done.104) | copy-start | bytes 5380
  1249.8 117.9 %copy-start.112 = (f32[64,4]{0,1:T(4,128)S(1)}, f32[64,4]{0,1:T(4,128)}, u32[]{:S(2)}) copy-start(f32[64,4]{0,1:T(4,128)} %copy-done.111) | copy-start | bytes 3076
  1249.8 117.9 %copy-start.114 = (f32[64,4]{0,1:T(4,128)S(1)}, f32[64,4]{0,1:T(4,128)}, u32[]{:S(2)}) copy-start(f32[64,4]{0,1:T(4,128)} %copy-done.113) | copy-start | bytes 3076
  1249.8 117.9 %copy-start.119 = (f32[64,3]{0,1:T(4,128)S(1)}, f32[64,3]{0,1:T(4,128)}, u32[]{:S(2)}) copy-start(f32[64,3]{0,1:T(4,128)} %copy-done.118) | copy-start | bytes 2308
  1249.8 118.1 %copy-start.137 = (f32[64,2]{0,1:T(2,128)S(1)}, f32[64,2]{0,1:T(2,128)}, u32[]{:S(2)}) copy-start(f32[64,2]{0,1:T(2,128)} %copy-done.136) | copy-start | bytes 1540
  1249.9 118.1 %copy-start.139 = (f32[64,2]{0,1:T(2,128)S(1)}, f32[64,2]{0,1:T(2,128)}, u32[]{:S(2)}) copy-start(f32[64,2]{0,1:T(2,128)} %copy-done.138) | copy-start | bytes 1540
  1249.9 118.8 %copy-start.131 = (f32[64,2]{0,1:T(2,128)S(1)}, f32[64,2]{0,1:T(2,128)}, u32[]{:S(2)}) copy-start(f32[64,2]{0,1:T(2,128)} %copy-done.130) | copy-start | bytes 1540
  1249.9 118.8 %copy-start.133 = (f32[64,2]{0,1:T(2,128)S(1)}, f32[64,2]{0,1:T(2,128)}, u32[]{:S(2)}) copy-start(f32[64,2]{0,1:T(2,128)} %copy-done.132) | copy-start | bytes 1540
  1249.9 118.8 %copy-start.135 = (f32[64,2]{0,1:T(2,128)S(1)}, f32[64,2]{0,1:T(2,128)}, u32[]{:S(2)}) copy-start(f32[64,2]{0,1:T(2,128)} %copy-done.134) | copy-start | bytes 1540
  1249.9 119.6 %copy-start.116 = (f32[64,4]{0,1:T(4,128)S(1)}, f32[64,4]{0,1:T(4,128)}, u32[]{:S(2)}) copy-start(f32[64,4]{0,1:T(4,128)} %copy-done.115) | copy-start | bytes 3076
  1249.9 119.6 %copy-start.121 = (f32[64,4]{0,1:T(4,128)S(1)}, f32[64,4]{0,1:T(4,128)}, u32[]{:S(2)}) copy-start(f32[64,4]{0,1:T(4,128)} %copy-done.120) | copy-start | bytes 3076
  1249.9 119.6 %copy-start.123 = (f32[64,4]{0,1:T(4,128)S(1)}, f32[64,4]{0,1:T(4,128)}, u32[]{:S(2)}) copy-start(f32[64,4]{0,1:T(4,128)} %copy-done.122) | copy-start | bytes 3076
  1249.9 119.6 %copy-start.125 = (f32[64,4]{0,1:T(4,128)S(1)}, f32[64,4]{0,1:T(4,128)}, u32[]{:S(2)}) copy-start(f32[64,4]{0,1:T(4,128)} %copy-done.124) | copy-start | bytes 3076
  1249.9 119.7 %copy-start.79 = (f32[64,8]{0,1:T(8,128)S(1)}, f32[64,8]{0,1:T(8,128)}, u32[]{:S(2)}) copy-start(f32[64,8]{0,1:T(8,128)} %copy-done.78) | copy-start | bytes 6148
  1250.0 119.7 %copy-start.99 = (f32[64,8]{0,1:T(8,128)S(1)}, f32[64,8]{0,1:T(8,128)}, u32[]{:S(2)}) copy-start(f32[64,8]{0,1:T(8,128)} %copy-done.98) | copy-start | bytes 6148
  1250.0 119.7 %copy-start.101 = (f32[64,8]{0,1:T(8,128)S(1)}, f32[64,8]{0,1:T(8,128)}, u32[]{:S(2)}) copy-start(f32[64,8]{0,1:T(8,128)} %copy-done.100) | copy-start | bytes 6148
  1250.0 119.7 %copy-start.103 = (f32[64,8]{0,1:T(8,128)S(1)}, f32[64,8]{0,1:T(8,128)}, u32[]{:S(2)}) copy-start(f32[64,8]{0,1:T(8,128)} %copy-done.102) | copy-start | bytes 6148
  1250.0 119.9 %copy-start.57 = (f32[64,16]{0,1:T(8,128)S(1)}, f32[64,16]{0,1:T(8,128)}, u32[]{:S(2)}) copy-start(f32[64,16]{0,1:T(8,128)} %copy-done.56) | copy-start | bytes 12292
  1250.0 119.9 %copy-start.67 = (f32[64,16]{0,1:T(8,128)S(1)}, f32[64,16]{0,1:T(8,128)}, u32[]{:S(2)}) copy-start(f32[64,16]{0,1:T(8,128)} %copy-done.66) | copy-start | bytes 12292
  1250.0 119.9 %copy-start.69 = (f32[64,16]{0,1:T(8,128)S(1)}, f32[64,16]{0,1:T(8,128)}, u32[]{:S(2)}) copy-start(f32[64,16]{0,1:T(8,128)} %copy-done.68) | copy-start | bytes 12292
  1250.0 119.9 %copy-start.71 = (f32[64,16]{0,1:T(8,128)S(1)}, f32[64,16]{0,1:T(8,128)}, u32[]{:S(2)}) copy-start(f32[64,16]{0,1:T(8,128)} %copy-done.70) | copy-start | bytes 12292
  1250.0 120.6 %copy-start.50 = (f32[64,32]{0,1:T(8,128)S(1)}, f32[64,32]{0,1:T(8,128)}, u32[]{:S(2)}) copy-start(f32[64,32]{0,1:T(8,128)} %copy-done.49) | copy-start | bytes 24580
  1250.0 121.1 %copy-start.48 = (f32[64,32]{0,1:T(8,128)S(1)}, f32[64,32]{0,1:T(8,128)}, u32[]{:S(2)}) copy-start(f32[64,32]{0,1:T(8,128)} %copy-done.47) | copy-start | bytes 24580
  1253.9 117.8 %copy-start.152 = (f32[64]{0:T(128)S(1)}, f32[64]{0:T(128)}, u32[]{:S(2)}) copy-start(f32[64]{0:T(128)} %copy-done.151) | copy-start | bytes 772
  1485.2 131.5 %all-reduce.93.cloned.1.call-start = ((), (), s32[]{:S(2)}) async-start(), calls=%async_computation.15 | async-start | bytes 3407872 | tf_op jit(solution)/shard_map/psum | solution.py:257
  1490.9 306.4 %reduce-scatter.11.cloned.1.call-start = ((), (), s32[]{:S(2)}) async-start(), calls=%async_computation.13 | async-start | bytes 8912896 | tf_op jit(solution)/shard_map/reduce_scatter | solution.py:248
  1501.3 298.2 %copy-start.1 = (bf16[256,1024]{1,0:T(8,128)(2,1)S(1)}, bf16[256,1024]{1,0:T(8,128)(2,1)}, u32[]{:S(2)}) copy-start(bf16[256,1024]{1,0:T(8,128)(2,1)} %param.40) | copy-start | bytes 1572868
  1501.5 295.8 %copy-start.10 = (f32[256,1024]{1,0:T(8,128)S(1)}, f32[256,1024]{1,0:T(8,128)}, u32[]{:S(2)}) copy-start(f32[256,1024]{1,0:T(8,128)} %copy-done.9) | copy-start | bytes 3145732
  1501.5 295.8 %copy-start.20 = (bf16[256,1024]{1,0:T(8,128)(2,1)S(1)}, bf16[256,1024]{1,0:T(8,128)(2,1)}, u32[]{:S(2)}) copy-start(bf16[256,1024]{1,0:T(8,128)(2,1)} %param.22) | copy-start | bytes 1572868
  1501.5 295.8 %copy-start.129 = (f32[256]{0:T(256)S(1)}, f32[256]{0:T(256)}, u32[]{:S(2)}) copy-start(f32[256]{0:T(256)} %copy-done.128) | copy-start | bytes 3076
  (128 other events, 2726.1 us)
Sparse Core Ops, SparseCore 0:
  10.8 114.1 all-gather.4
  199.9 345.3 reduce-scatter.4
  548.9 117.6 all-gather.6
  694.9 187.9 reduce-scatter.6
  886.1 123.1 all-gather.8
  1053.9 176.5 reduce-scatter.8
  1237.0 114.6 all-gather.10
  1485.3 104.5 all-reduce.90
  1594.1 22.5 all-reduce.92
  1618.9 178.4 reduce-scatter.10
where the time goes:
time: 1820 us; the launch traced here: 1810 us
  waiting for transfers between devices  1350 us (74%)
  other arithmetic  210 us (12%)
  matrix products  138 us (8%)
  blocking collectives  41.8 us (2%)
  local copies, waits for them, and re-layouts  26.9 us (1%)
  starting transfers between devices  18.4 us (1%)
    reduce_scatter x1, waiting for transfers between devices, shards(): lax.psum_scatter(jnp.dot(gated, weight_output, preferred_element_type=jnp...  345 us
    reduce_scatter x1, waiting for transfers between devices, shards(): lax.psum_scatter(grad_second_part.astype(jnp.bfloat16), 'mp', scatter_dim...  177 us
    reduce_scatter x1, waiting for transfers between devices, shards(): lax.psum_scatter(grad_raw.astype(jnp.bfloat16), 'mp', scatter_dimension=0...  168 us
    reduce_scatter x1, waiting for transfers between devices, shards(): lax.psum_scatter(jnp.dot(squared, hidden_value, preferred_element_type=jn...  133 us
    all_gather x1, waiting for transfers between devices, shards(): wide_rows = lax.all_gather(second_low, 'mp', axis=0, tiled=True)  116 us
    all_gather x1, waiting for transfers between devices, shards(): gathered = lax.all_gather(tokens, 'mp', axis=0, tiled=True)  113 us
    all_gather x1, waiting for transfers between devices, shards(): grad_att_all = lax.all_gather(grad_attended, 'mp', axis=0, tiled=True)  97.8 us
    all_gather x1, waiting for transfers between devices, shards(): grad_wide = lax.all_gather(grad_carried, 'mp', axis=0, tiled=True)  85.7 us
  transfers between devices with their start and end apart: 11, of which 11 were waited for; matrix products, arithmetic and copies ran while one was open for 4% of the time, Pallas kernels for 0%

commit v1 on v0

v1 whole, which is shorter than its diff:
```python
import functools

import jax
import jax.numpy as jnp
from jax import lax
from jax.experimental import pallas as pl
from jax.experimental.pallas import tpu as pltpu
from jax.sharding import PartitionSpec as P

norm_eps = 1e-05
f32 = jnp.float32
bf16 = jnp.bfloat16


def bits_of(count):
    total = count.bit_length() - 1
    cube = (0, 2, 4) if total == 5 else (0, 1, 2)
    pre = tuple(b for b in range(total) if b not in cube)
    return pre, cube


def swap(value, bit):
    count = lax.axis_size("mp")
    return lax.ppermute(value, "mp", [(i, i ^ (1 << bit)) for i in range(count)])


def swap_core(value):
    count = lax.axis_size("dp")
    return lax.ppermute(value, "dp", [(i, i ^ 1) for i in range(count)])


def relative_ids(count):
    pre, (a, b, c) = bits_of(count)
    low = [0]
    for bit in pre:
        low = low + [i ^ (1 << bit) for i in low]
    x, y, z = 1 << a, 1 << b, 1 << c
    return [k ^ i for k in (0, x, y, z, x ^ y, y ^ z, x ^ z, x ^ y ^ z) for i in low]


def gather_chunk(part):
    pre, (a, b, c) = bits_of(lax.axis_size("mp"))
    v = part[None]
    for bit in pre:
        v = jnp.concatenate([v, swap(v, bit)], 0)
    vx, vy, vz = swap(v, a), swap(v, b), swap(v, c)
    xy, yz, xz = swap(vy, a), swap(vz, b), swap(vx, c)
    half = v.shape[0] // 2
    one, two = swap(yz[:half], a), swap(xz[half:], b)
    return jnp.concatenate([v, vx, vy, vz, xy, yz, xz, one, two], 0)


def scatter_chunk(part):
    count = lax.axis_size("mp")
    pre, (a, b, c) = bits_of(count)
    p = part.reshape((8, count // 8) + part.shape[1:])
    half = p.shape[1] // 2
    one, two = swap(p[7, :half], a), swap(p[7, half:], b)
    yz = jnp.concatenate([p[5, :half] + one, p[5, half:]], 0)
    xz = jnp.concatenate([p[6, :half], p[6, half:] + two], 0)
    y = p[2] + swap(p[4], a)
    z = p[3] + swap(yz, b)
    x = p[1] + swap(xz, c)
    v = p[0] + swap(x, a) + swap(y, b) + swap(z, c)
    for bit in reversed(pre):
        half = v.shape[0] // 2
        v = v[:half] + swap(v[half:], bit)
    return v[0]


def gather_small(value):
    count = lax.axis_size("mp")
    v = value[None]
    for bit in range(count.bit_length() - 1):
        v = jnp.concatenate([v, swap(v, bit)], 0)
    return v


def total_small(value):
    for axis in ("mp", "dp"):
        count = lax.axis_size(axis)
        for bit in range(count.bit_length() - 1):
            value = value + lax.ppermute(value, axis, [(i, i ^ (1 << bit)) for i in range(count)])
    return value


ANY = pl.BlockSpec(memory_space=pl.ANY)
SMEM = pl.BlockSpec(memory_space=pltpu.SMEM)


def place_kernel(pieces, count, places_ref, own_ref, other_ref, *rest):
    outs, sem = rest[:-1], rest[-1]
    copies = []
    for (offset, rows), out in zip(pieces, outs):
        for side, source in enumerate((own_ref, other_ref)):
            for j in range(count):
                target = pl.multiple_of(places_ref[side, j] * rows, 16)
                copies.append(
                    pltpu.make_async_copy(
                        source.at[j, pl.ds(offset, rows), :],
                        out.at[pl.ds(target, rows), :],
                        sem.at[len(copies)],
                    )
                )
    for copy in copies:
        copy.start()
    for copy in copies:
        copy.wait()


def place(own, other, places, pieces):
    count, _, width = own.shape
    return pl.pallas_call(
        functools.partial(place_kernel, pieces, count),
        out_shape=tuple(
            jax.ShapeDtypeStruct((2 * count * rows, width), own.dtype) for _, rows in pieces
        ),
        in_specs=[SMEM, ANY, ANY],
        out_specs=tuple(ANY for _ in pieces),
        scratch_shapes=[pltpu.SemaphoreType.DMA((2 * count * len(pieces),))],
    )(places, own, other)


def unplace_kernel(pieces, count, places_ref, *rest):
    sources, (own_ref, other_ref, sem) = rest[:-3], rest[-3:]
    copies = []
    for (offset, rows), source in zip(pieces, sources):
        for side, out in enumerate((own_ref, other_ref)):
            for j in range(count):
                start = pl.multiple_of(places_ref[side, j] * rows, 16)
                copies.append(
                    pltpu.make_async_copy(
                        source.at[pl.ds(start, rows), :],
                        out.at[j, pl.ds(offset, rows), :],
                        sem.at[len(copies)],
                    )
                )
    for copy in copies:
        copy.start()
    for copy in copies:
        copy.wait()


def unplace(matrices, places, pieces, count):
    width = matrices[0].shape[1]
    height = sum(rows for _, rows in pieces)
    shape = jax.ShapeDtypeStruct((count, height, width), matrices[0].dtype)
    return pl.pallas_call(
        functools.partial(unplace_kernel, pieces, count),
        out_shape=(shape, shape),
        in_specs=[SMEM] + [ANY] * len(matrices),
        out_specs=(ANY, ANY),
        scratch_shapes=[pltpu.SemaphoreType.DMA((2 * count * len(pieces),))],
    )(places, *matrices)


def tile_down(value_a, value_b, cols, powers):
    for k in range(3):
        factor = powers[k] * cols[:, k : k + 1]
        value_a = value_a + factor * pltpu.roll(value_a, 1 << k, 0)
        value_b = value_b + factor * pltpu.roll(value_b, 1 << k, 0)
    return value_a, value_b


def tile_up(value_a, value_b, cols, powers):
    for k in range(3):
        factor = powers[k] * cols[:, k : k + 1]
        value_a = value_a + factor * pltpu.roll(value_a, 8 - (1 << k), 0)
        value_b = value_b + factor * pltpu.roll(value_b, 8 - (1 << k), 0)
    return value_a, value_b


def forward_end_kernel(k_ref, v_ref, cols_ref, decay_ref, out_ref):
    rows, width = k_ref.shape
    rate = jnp.exp(decay_ref[0:1, :])
    powers = [jnp.exp(-rate * (1 << k)) for k in range(3)]
    climb = lax.broadcasted_iota(jnp.int32, (8, width), 0).astype(f32) + 1.0
    full = jnp.exp(-rate * climb)

    def body(t, carry):
        at = pl.ds(pl.multiple_of(t * 8, 8), 8)
        cols = cols_ref[at, :]
        growth = jnp.exp(k_ref[at, :])
        ya, yb = tile_down(growth * v_ref[at, :], growth, cols, powers)
        reach = full * cols[:, 3:4]
        ya = ya + reach * carry[0]
        yb = yb + reach * carry[1]
        return ya[7:8, :], yb[7:8, :]

    zero = jnp.zeros((1, width), f32)
    ya, yb = lax.fori_loop(0, rows // 8, body, (zero, zero))
    out_ref[0:1, :] = ya
    out_ref[1:2, :] = yb


def forward_kernel(k_ref, v_ref, r_ref, cols_ref, decay_ref, enter_ref, gated_ref, mixed_ref, a_ref, b_ref):
    rows, width = k_ref.shape
    rate = jnp.exp(decay_ref[0:1, :])
    bonus = decay_ref[1:2, :]
    powers = [jnp.exp(-rate * (1 << k)) for k in range(3)]
    place_in = lax.broadcasted_iota(jnp.int32, (8, width), 0)
    full = jnp.exp(-rate * (place_in.astype(f32) + 1.0))

    def body(t, carry):
        at = pl.ds(pl.multiple_of(t * 8, 8), 8)
        cols = cols_ref[at, :]
        keys = k_ref[at, :]
        values = v_ref[at, :]
        growth = jnp.exp(keys)
        ya, yb = tile_down(growth * values, growth, cols, powers)
        reach = full * cols[:, 3:4]
        ya = ya + reach * carry[0]
        yb = yb + reach * carry[1]
        keep = cols[:, 4:5]
        sa = keep * jnp.where(place_in == 0, carry[0], pltpu.roll(ya, 1, 0))
        sb = keep * jnp.where(place_in == 0, carry[1], pltpu.roll(yb, 1, 0))
        now = jnp.exp(bonus + keys)
        mixed = (sa + now * values) / (sb + now)
        a_ref[at, :] = sa
        b_ref[at, :] = sb
        mixed_ref[at, :] = mixed
        gated_ref[at, :] = jax.nn.sigmoid(r_ref[at, :]) * mixed
        return ya[7:8, :], yb[7:8, :]

    lax.fori_loop(0, rows // 8, body, (enter_ref[0:1, :], enter_ref[1:2, :]))


def backward_end_kernel(g_ref, k_ref, mixed_ref, b_ref, cols_ref, decay_ref, out_ref):
    rows, width = k_ref.shape
    rate = jnp.exp(decay_ref[0:1, :])
    bonus = decay_ref[1:2, :]
    powers = [jnp.exp(-rate * (1 << k)) for k in range(3)]
    place_in = lax.broadcasted_iota(jnp.int32, (8, width), 0)
    full = jnp.exp(-rate * (8.0 - place_in.astype(f32)))
    tiles = rows // 8

    def body(step, carry):
        at = pl.ds(pl.multiple_of((tiles - 1 - step) * 8, 8), 8)
        cols = cols_ref[at, :]
        now = jnp.exp(bonus + k_ref[at, :])
        xa = g_ref[at, :] / (b_ref[at, :] + now)
        ya, yb = tile_up(xa, -xa * mixed_ref[at, :], cols, powers)
        reach = full * cols[:, 3:4]
        ya = ya + reach * carry[0]
        yb = yb + reach * carry[1]
        return ya[0:1, :], yb[0:1, :]

    zero = jnp.zeros((1, width), f32)
    ya, yb = lax.fori_loop(0, tiles, body, (zero, zero))
    out_ref[0:1, :] = ya
    out_ref[1:2, :] = yb


def backward_kernel(
    g_ref, k_ref, v_ref, mixed_ref, a_ref, b_ref, cols_ref, decay_ref, enter_ref, gk_ref, gv_ref, small_ref
):
    rows, width = k_ref.shape
    rate = jnp.exp(decay_ref[0:1, :])
    bonus = decay_ref[1:2, :]
    powers = [jnp.exp(-rate * (1 << k)) for k in range(3)]
    place_in = lax.broadcasted_iota(jnp.int32, (8, width), 0)
    full = jnp.exp(-rate * (8.0 - place_in.astype(f32)))
    tiles = rows // 8

    def body(step, carry):
        at = pl.ds(pl.multiple_of((tiles - 1 - step) * 8, 8), 8)
        cols = cols_ref[at, :]
        keys = k_ref[at, :]
        values = v_ref[at, :]
        mixed = mixed_ref[at, :]
        sa, sb = a_ref[at, :], b_ref[at, :]
        now = jnp.exp(bonus + keys)
        growth = jnp.exp(keys)
        xa = g_ref[at, :] / (sb + now)
        ya, yb = tile_up(xa, -xa * mixed, cols, powers)
        reach = full * cols[:, 3:4]
        ya = ya + reach * carry[0]
        yb = yb + reach * carry[1]
        keep = cols[:, 4:5]
        after_a = keep * jnp.where(place_in == 7, carry[0], pltpu.roll(ya, 7, 0))
        after_b = keep * jnp.where(place_in == 7, carry[1], pltpu.roll(yb, 7, 0))
        share = xa * now
        bend = share * (values - mixed)
        gv_ref[at, :] = share + after_a * growth
        gk_ref[at, :] = bend + growth * (after_a * values + after_b)
        return (
            ya[0:1, :],
            yb[0:1, :],
            carry[2] + bend,
            carry[3] + after_a * sa + after_b * sb,
        )

    zero = jnp.zeros((8, width), f32)
    done = lax.fori_loop(0, tiles, body, (enter_ref[0:1, :], enter_ref[1:2, :], zero, zero))
    small_ref[0:1, :] = jnp.sum(done[3], axis=0, keepdims=True) * (-rate * jnp.exp(-rate))
    small_ref[1:2, :] = jnp.sum(done[2], axis=0, keepdims=True)


def call_whole(kernel, outs, *args):
    return pl.pallas_call(
        kernel,
        out_shape=outs,
        in_specs=[pl.BlockSpec(memory_space=pltpu.VMEM)] * len(args),
        out_specs=jax.tree.map(lambda _: pl.BlockSpec(memory_space=pltpu.VMEM), outs),
        compiler_params=pltpu.CompilerParams(vmem_limit_bytes=40 * 2**20),
    )(*args)


def dot(left, right):
    return jnp.dot(left, right, preferred_element_type=f32)


def outer_sum(left, right):
    return lax.dot_general(left, right, (((0,), (0,)), ((), ())), preferred_element_type=f32)


def against(left, weight):
    return lax.dot_general(left, weight, (((1,), (1,)), ((), ())), preferred_element_type=f32)


def normalize(source):
    centre = jnp.mean(source, axis=-1, keepdims=True)
    spread = source - centre
    inverse = lax.rsqrt(jnp.mean(spread * spread, axis=-1, keepdims=True) + norm_eps)
    return spread * inverse, inverse


def blend_pair(present, before, factor):
    return (present.astype(f32) * factor + before * (1.0 - factor)).astype(bf16)


def norm_back(grad, scaled, inverse, gain):
    h = grad * gain
    return inverse * (
        h
        - jnp.mean(h, axis=-1, keepdims=True)
        - scaled * jnp.mean(h * scaled, axis=-1, keepdims=True)
    )


def shards(
    tokens,
    cotangent,
    seq_lengths,
    first_gain,
    first_bias,
    second_gain,
    second_bias,
    blend_key,
    blend_value,
    blend_recept,
    channel_key,
    channel_recept,
    time_decay,
    time_first,
    weight_key,
    weight_value,
    weight_recept,
    weight_output,
    hidden_key,
    hidden_value,
    hidden_recept,
):
    count = lax.axis_size("mp")
    me = lax.axis_index("mp")
    core = lax.rem(lax.axis_index("dp"), 2)
    rows, width = tokens.shape
    group_rows = rows * count
    chan = weight_key.shape[1]
    units = hidden_key.shape[1]
    hc, hu = chan // 2, units // 2
    ids = relative_ids(count)
    shift_down = [(i, i + 1) for i in range(count - 1)]
    shift_up = [(i + 1, i) for i in range(count - 1)]

    def half_rows(matrix, size):
        return lax.dynamic_slice_in_dim(matrix, core * size, size, 0)

    def half_cols(matrix, size):
        return lax.dynamic_slice_in_dim(matrix, core * size, size, 1).T

    chunk_a = jnp.concatenate(
        [
            half_cols(weight_key, hc),
            half_cols(weight_value, hc),
            half_cols(weight_recept, hc),
            half_rows(weight_output, hc),
        ],
        0,
    )
    chunk_b = jnp.concatenate([half_cols(hidden_key, hu), half_cols(hidden_recept, hc)], 0)
    chunk_c = half_rows(hidden_value, hu)
    own_a = gather_chunk(chunk_a)
    own_b = gather_chunk(chunk_b)
    own_c = gather_chunk(chunk_c)
    other_a, other_b, other_c = swap_core(own_a), swap_core(own_b), swap_core(own_c)
    ids_array = jnp.array(ids, jnp.int32)
    owners = jnp.bitwise_xor(ids_array, me)
    places = jnp.stack([owners * 2 + core, owners * 2 + 1 - core]).astype(jnp.int32)

    lengths = seq_lengths[0]
    ends = jnp.cumsum(lengths)

    def start_of(place):
        return jnp.sum(jnp.where(ends <= place[..., None], lengths, 0), axis=-1)

    def keep_of(place):
        return ((place > start_of(place)) & (place < group_rows)).astype(f32)

    here = me * rows + jnp.arange(rows, dtype=jnp.int32)
    keep_flat = keep_of(here)
    keep = keep_flat[:, None]
    keep_next = keep_of(here + 1)
    tiles = rows // 8

    def tile_cols(flags, up):
        f = flags.reshape(tiles, 8)
        if up:
            f = f[:, ::-1]
        one = f * (jnp.arange(8) >= 1)
        two = f * jnp.roll(f, 1, 1) * (jnp.arange(8) >= 2)
        four = f * jnp.roll(f, 1, 1) * jnp.roll(f, 2, 1) * jnp.roll(f, 3, 1) * (jnp.arange(8) >= 4)
        through = jnp.cumprod(f, axis=1)
        cols = jnp.stack([one, two, four, through, f, f, f, f], axis=-1)
        if up:
            cols = cols[:, ::-1]
        return cols.reshape(rows, 8)

    cols_down = tile_cols(keep_flat, False)
    cols_up = tile_cols(keep_next, True)

    small_rates = gather_small(jnp.stack([time_decay, time_first]))
    order = jnp.bitwise_xor(jnp.arange(count, dtype=jnp.int32), me)
    rates = jnp.moveaxis(jnp.take(small_rates, order, axis=0), 0, 1).reshape(2, width)
    rate = jnp.exp(rates[0])

    source = tokens.astype(f32)
    edge_row = lax.ppermute(tokens[-1:], "mp", shift_down).astype(f32)
    scaled_one, inverse_one = normalize(source)
    normed = (scaled_one * first_gain + first_bias).astype(bf16)
    edge = (normalize(edge_row)[0] * first_gain + first_bias).astype(bf16)
    before = jnp.concatenate([edge, normed[:-1]], 0).astype(f32) * keep
    mix_key = blend_pair(normed, before, blend_key)
    mix_value = blend_pair(normed, before, blend_value)
    mix_recept = blend_pair(normed, before, blend_recept)

    key_t, value_t, recept_t, output_w = place(
        own_a, other_a, places, ((0, hc), (hc, hc), (2 * hc, hc), (3 * hc, hc))
    )
    keys = against(mix_key, key_t)
    values = against(mix_value, value_t)
    recept = against(mix_recept, recept_t)

    pair = jax.ShapeDtypeStruct((2, width), f32)
    field = jax.ShapeDtypeStruct((rows, width), f32)
    sources = jnp.bitwise_xor(jnp.arange(count, dtype=jnp.int32), me)

    def fold(ends_all, valid, distance):
        weight = jnp.where(
            valid[:, None], jnp.exp(-rate[None] * (rows * distance[:, None]).astype(f32)), 0.0
        )
        return jnp.sum(ends_all * weight[:, None], axis=0)

    out_end = call_whole(forward_end_kernel, pair, keys, values, cols_down, rates)
    enter = fold(
        gather_small(out_end),
        (sources < me) & (start_of(me * rows - 1) < rows * (sources + 1)),
        jnp.maximum(me - 1 - sources, 0),
    )
    gated_full, mixed, state_a, state_b = call_whole(
        forward_kernel, (field, field, field, field), keys, values, recept, cols_down, rates, enter
    )
    gated = gated_full.astype(bf16)
    opened = jax.nn.sigmoid(recept)

    hidden = source + dot(gated, output_w)
    scaled_two, inverse_two = normalize(hidden)
    low = (scaled_two * second_gain + second_bias).astype(bf16)
    edge_two = lax.ppermute(low[-1:], "mp", shift_down)
    prior = jnp.concatenate([edge_two, low[:-1]], 0).astype(f32) * keep
    ffn_key_in = blend_pair(low, prior, channel_key)
    ffn_recept_in = blend_pair(low, prior, channel_recept)
    (hidden_recept_t,) = place(own_b, other_b, places, ((hu, hc),))
    hidden_key_t = jnp.concatenate([own_b[:, :hu], other_b[:, :hu]], 0).reshape(-1, width)
    hidden_value_w = jnp.concatenate([own_c, other_c], 0).reshape(-1, width)
    ffn_relu = jax.nn.relu(against(ffn_key_in, hidden_key_t))
    squared = jnp.square(ffn_relu).astype(bf16)
    gate = jax.nn.sigmoid(against(ffn_recept_in, hidden_recept_t))
    grad_out = cotangent.astype(f32)
    grad_carried = (grad_out * gate).astype(bf16)

    def split(matrix, size):
        parts = matrix.astype(bf16).reshape(2, count, size, width)
        return parts[0], parts[1]

    def reduce_chunk(own, other):
        return scatter_chunk(own + swap_core(other))

    g_value_own, g_value_other = split(outer_sum(squared, grad_carried), hu)
    sum_c = reduce_chunk(g_value_own, g_value_other)

    carried = dot(squared, hidden_value_w)
    block_out = (hidden + gate * carried).astype(bf16)
    grad_gate_pre = (grad_out * carried * gate * (1.0 - gate)).astype(bf16)
    grad_pre = (against(grad_carried, hidden_value_w) * 2.0 * ffn_relu).astype(bf16)
    g_key_own, g_key_other = split(outer_sum(grad_pre, ffn_key_in), hu)
    g_recept_own, g_recept_other = unplace(
        [outer_sum(grad_gate_pre, ffn_recept_in).astype(bf16)], places, ((0, hc),), count
    )
    sum_b = reduce_chunk(
        jnp.concatenate([g_key_own, g_recept_own], 1), jnp.concatenate([g_key_other, g_recept_other], 1)
    )
    grad_key_two = dot(grad_pre, hidden_key_t)
    grad_recept_two = dot(grad_gate_pre, hidden_recept_t)

    def blend_back(present, earlier, grads, factors):
        direct = sum(g * f for g, f in zip(grads, factors))
        spill = sum(g * (1.0 - f) for g, f in zip(grads, factors)) * keep
        tail = lax.ppermute(spill[:1], "mp", shift_up)
        change = present.astype(f32) - earlier
        totals = [jnp.sum(g * change, axis=0) for g in grads]
        return direct + jnp.concatenate([spill[1:], tail], 0), totals

    grad_second, ffn_small = blend_back(
        low, prior, (grad_key_two, grad_recept_two), (channel_key, channel_recept)
    )
    grad_second_gain = jnp.sum(grad_second * scaled_two, axis=0)
    grad_second_bias = jnp.sum(grad_second, axis=0)
    grad_hidden = grad_out + norm_back(grad_second, scaled_two, inverse_two, second_gain)
    grad_attended = grad_hidden.astype(bf16)

    g_output = outer_sum(gated, grad_attended).astype(bf16)
    grad_gated = against(grad_attended, output_w)
    grad_mixed = grad_gated * opened
    grad_recept = (grad_gated * mixed * opened * (1.0 - opened)).astype(bf16)
    back_end = call_whole(
        backward_end_kernel, pair, grad_mixed, keys, mixed, state_b, cols_up, rates
    )
    enter_back = fold(
        gather_small(back_end),
        (sources > me) & (start_of(sources * rows) <= rows * (me + 1)),
        jnp.maximum(sources - 1 - me, 0),
    )
    grad_keys_full, grad_values_full, rate_small = call_whole(
        backward_kernel,
        (field, field, pair),
        grad_mixed,
        keys,
        values,
        mixed,
        state_a,
        state_b,
        cols_up,
        rates,
        enter_back,
    )
    grad_keys = grad_keys_full.astype(bf16)
    grad_values = grad_values_full.astype(bf16)
    g_key = outer_sum(grad_keys, mix_key).astype(bf16)
    g_value = outer_sum(grad_values, mix_value).astype(bf16)
    g_recept = outer_sum(grad_recept, mix_recept).astype(bf16)
    sum_a = reduce_chunk(
        *unplace(
            [g_key, g_value, g_recept, g_output],
            places,
            ((0, hc), (hc, hc), (2 * hc, hc), (3 * hc, hc)),
            count,
        )
    )
    grad_key_one = dot(grad_keys, key_t)
    grad_value_one = dot(grad_values, value_t)
    grad_recept_one = dot(grad_recept, recept_t)
    grad_normed, mixer_small = blend_back(
        normed,
        before,
        (grad_key_one, grad_value_one, grad_recept_one),
        (blend_key, blend_value, blend_recept),
    )
    grad_first_gain = jnp.sum(grad_normed * scaled_one, axis=0)
    grad_first_bias = jnp.sum(grad_normed, axis=0)
    grad_tokens = grad_hidden + norm_back(grad_normed, scaled_one, inverse_one, first_gain)

    small = total_small(
        jnp.stack(
            [
                grad_first_gain,
                grad_first_bias,
                grad_second_gain,
                grad_second_bias,
                *mixer_small,
                *ffn_small,
                rate_small[0],
                rate_small[1],
            ]
        )
    )
    mine = lax.dynamic_slice_in_dim(small[9:], me * chan, chan, 1)

    def finish(part):
        size = lax.axis_size("dp")
        step = 2
        while step < size:
            part = part + lax.ppermute(part, "dp", [(i, i ^ step) for i in range(size)])
            step *= 2
        far = swap_core(part)
        first = jnp.where(core == 0, part, far)
        second = jnp.where(core == 0, far, part)

        def take(offset, length):
            return jnp.concatenate(
                [first[offset : offset + length], second[offset : offset + length]], 0
            ).astype(f32)

        return take

    take_a, take_b, take_c = finish(sum_a), finish(sum_b), finish(sum_c)
    return (
        block_out,
        grad_tokens,
        small[0],
        small[1],
        small[2],
        small[3],
        small[4],
        small[5],
        small[6],
        small[7],
        small[8],
        mine[0],
        mine[1],
        take_a(0, hc).T,
        take_a(hc, hc).T,
        take_a(2 * hc, hc).T,
        take_a(3 * hc, hc),
        take_b(0, hu).T,
        take_c(0, hu),
        take_b(hu, hc).T,
    )


def solution(mesh):
    rows = P(("dp", "mp"), None)
    cols = P(None, "mp")
    tall = P("mp", None)
    each = P("mp")
    return jax.shard_map(
        shards,
        mesh=mesh,
        in_specs=(rows, rows, P("dp", None))
        + (P(),) * 9
        + (each, each, cols, cols, cols, tall, cols, tall, cols),
        out_specs=(rows, rows) + (P(),) * 9 + (each, each, cols, cols, cols, tall, cols, tall, cols),
        check_vma=False,
    )
```

time: 1820 us -> 1150 us (0.63)
  waiting for transfers between devices: 1350 us -> 150 us
  Pallas kernels: 0 us -> 660 us
  other arithmetic: 210 us -> 58.9 us
  starting transfers between devices: 18.4 us -> 133 us
  matrix products: 138 us -> 64 us
  local copies, waits for them, and re-layouts: 26.9 us -> 74.8 us
  blocking collectives: 41.8 us -> 0 us
    reduce_scatter x4 -> x0, waiting for transfers between devices: 824 us -> none  [the longest x1 345 us: shards(): lax.psum_scatter(jnp.dot(gated, weight_output, preferred_element_type=jnp...]
    pallas_call x0 -> x8, Pallas kernels: none -> 660 us  [the longest x2 323 us: place(): pl.pallas_call(functools.partial(place_kernel, pieces, count), out_shape=...]
    all_gather x4 -> x0, waiting for transfers between devices: 413 us -> none  [the longest x1 116 us: shards(): wide_rows = lax.all_gather(second_low, 'mp', axis=0, tiled=True)]
    ppermute x0 -> x84, waiting for transfers between devices: none -> 150 us  [the longest x66 139 us: swap(): return lax.ppermute(value, 'mp', [(i, i ^ 1 << bit) for i in range(count)])]
    ppermute x0 -> x84, starting transfers between devices: none -> 133 us  [the longest x66 76.4 us: swap(): return lax.ppermute(value, 'mp', [(i, i ^ 1 << bit) for i in range(count)])]
    unnamed x11 -> x0, waiting for transfers between devices: 83.8 us -> none
    reduce_sum x19 -> x12, other arithmetic: 82.9 us -> 7.35 us  [the longest x1 3.01 us: shards(): grad_second_gain = jnp.sum(grad_second * scaled_two, axis=0)]
    convert_element_type x22 -> x12, other arithmetic: 74.9 us -> 2.43 us  [the longest x2 1.81 us: take(): return jnp.concatenate([first[offset:offset + length], second[offset:offs...]
  transfers between devices with their start and end apart: 11 -> 84, of which waited for: 11 -> 38; matrix products, arithmetic and copies ran while one was open for 4% -> 13% of each run, Pallas kernels for 0% -> 58%
where the time goes in v1:
time: 1150 us; the launch traced here: 1140 us
  Pallas kernels  660 us (57%)
  waiting for transfers between devices  150 us (13%)
  starting transfers between devices  133 us (12%)
  local copies, waits for them, and re-layouts  74.8 us (7%)
  matrix products  64 us (6%)
  other arithmetic  58.9 us (5%)
    pallas_call x2, Pallas kernels, place(): pl.pallas_call(functools.partial(place_kernel, pieces, count), out_shape=...  323 us
    pallas_call x2, Pallas kernels, unplace(): pl.pallas_call(functools.partial(unplace_kernel, pieces, count), out_shap...  323 us
    ppermute x66, waiting for transfers between devices, swap(): return lax.ppermute(value, 'mp', [(i, i ^ 1 << bit) for i in range(count)])  139 us
    ppermute x66, starting transfers between devices, swap(): return lax.ppermute(value, 'mp', [(i, i ^ 1 << bit) for i in range(count)])  76.4 us
    unnamed x163, local copies, waits for them, and re-layouts  38.8 us
    ppermute x9, starting transfers between devices, swap_core(): return lax.ppermute(value, 'dp', [(i, i ^ 1) for i in range(count)])  35.9 us
    dot_general x7, matrix products, dot(): return jnp.dot(left, right, preferred_element_type=f32)  27.7 us
  transfers between devices with their start and end apart: 84, of which 38 were waited for; matrix products, arithmetic and copies ran while one was open for 13% of the time, Pallas kernels for 58%

profile of v1, /device:TPU:1, one launch (start us, length us, event | category | flops | bytes accessed | tf_op | source)
XLA Modules:
  0.0 1144.6 jit_solution(4529669091034605519)
XLA Ops:
  3.5 3.2 collective-permute-start.1
  18.0 6.0 collective-permute-done.1
  28.9 12.8 %collective-permute-done.4 = bf16[2,128,1024]{2,1,0:T(8,128)(2,1)} collective-permute-done((bf16[2,128,1024]{2,1,0:T(8,128)(2,1)}, bf16[2,128,1024]{2,1,0:T(8,128)(2,1)}, u32[]{:S(2)}, u32[]{:S(2)}) %collective-permute-start.4) | collective-permute-done | bytes 524320 | tf_op jit(solution)/shard_map/ppermute | solution.py:24
  49.0 5.8 collective-permute-done.6
  61.8 6.8 collective-permute-done.5
  78.9 4.3 collective-permute-start.10
  83.2 4.0 collective-permute-done.20
  96.5 5.8 collective-permute-done.21
  110.3 6.3 collective-permute-start.39
  124.3 2.8 collective-permute-start.27
  134.6 5.5 collective-permute-start.29
  140.2 2.4 collective-permute-done.12
  145.3 3.0 collective-permute-start.14
  150.3 4.7 slice.454
  155.1 257.1 %shard_map.365 = (bf16[1024,1024]{1,0:T(8,128)(2,1)}, bf16[1024,1024]{1,0:T(8,128)(2,1)}, bf16[1024,1024]{1,0:T(8,128)(2,1)}, bf16[1024,1024]{1,0:T(8,128)(2,1)}) custom-call(s32[2,16]{1,0:T(2,128)} %pad_add_fusion.places_ref, bf16[16,128,1024]{2,1,0:T(8,128)(2,1)} %constant_dynamic-update-slice_fusion.own_ref, ...), custom_call_target="tpu_custom_call" | custom-call | tf_op jit(solution)/shard_map/pallas_call | solution.py:113
  412.1 2.6 fusion.93.k_ref
  415.6 3.3 shard_map.366
  419.9 5.2 constant_dynamic-update-slice_fusion.40
  430.7 2.4 collective-permute-start.18
  433.1 2.3 collective-permute-done.18
  435.6 4.0 shard_map.367
  444.4 3.6 collective-permute-start.19
  448.1 4.8 slice.455
  452.9 7.5 pad_maximum_fusion
  460.4 65.6 %shard_map.368 = bf16[1024,1024]{1,0:T(8,128)(2,1)} custom-call(s32[2,16]{1,0:T(2,128)} %pad_add_fusion.places_ref, bf16[16,160,1024]{2,1,0:T(8,128)(2,1)} %constant_dynamic-update-slice_fusion.20.own_ref, bf16[16,160,1024]{2,1,0:T(8,128)(2,1)} %collective-permute-done.29.other_ref), custom_call_target="tpu_custom_call" | custom-call | tf_op jit(solution)/shard_map/pallas_call | solution.py:113
  526.1 3.0 fusion.4
  530.6 2.5 convolution_maximum_fusion
  533.1 6.8 fusion.26
  540.0 5.9 fusion.1
  545.8 2.4 convolution_convert_fusion
  548.2 15.3 %fusion.106 = f32[256,1024]{1,0:T(8,128)S(1)} fusion(bf16[256,4096]{1,0:T(8,128)(2,1)S(1)} %fusion.1, bf16[4096,1024]{1,0:T(8,128)(2,1)} %bitcast.231), kind=kOutput, calls=%fused_computation.342 | convolution fusion | flops 2147483648 | bytes 11534336 | tf_op jit(solution)/shard_map/dot_general | solution.py:310
  566.6 3.7 fusion.100
  570.3 6.0 collective-permute-start.73
  576.4 6.0 convolution_convert_fusion.1
  585.7 65.6 %shard_map.372 = (bf16[16,32,1024]{2,1,0:T(8,128)(2,1)}, bf16[16,32,1024]{2,1,0:T(8,128)(2,1)}) custom-call(s32[2,16]{1,0:T(2,128)} %pad_add_fusion.places_ref, bf16[1024,1024]{1,0:T(8,128)(2,1)} %convolution_convert_fusion.2.rest_0_), custom_call_target="tpu_custom_call" | custom-call | tf_op jit(solution)/shard_map/pallas_call | solution.py:148
  651.4 3.0 multiply_reduce_fusion.5
  658.2 3.3 shard_map.369
  661.5 3.0 collective-permute-start.41
  664.5 2.4 convolution_convert_fusion.4.rest_2_
  673.4 3.0 collective-permute-start.44
  678.1 4.0 shard_map.370
  687.8 257.1 %shard_map.371 = (bf16[16,128,1024]{2,1,0:T(8,128)(2,1)}, bf16[16,128,1024]{2,1,0:T(8,128)(2,1)}) custom-call(s32[2,16]{1,0:T(2,128)} %pad_add_fusion.places_ref, bf16[1024,1024]{1,0:T(8,128)(2,1)} %convolution_convert_fusion.6.rest_0_, bf16[1024,1024]{1,0:T(8,128)(2,1)} %convolution_convert_fusion.5.rest_1_, ...), custom_call_target="tpu_custom_call" | custom-call | tf_op jit(solution)/shard_map/pallas_call | solution.py:148
  944.8 4.7 collective-permute-start.51
  949.6 5.4 fusion.101
  955.0 3.3 pad_maximum_fusion.1
  964.6 3.0 collective-permute-done.45
  978.1 2.9 collective-permute-start.49
  982.7 6.0 collective-permute-start.50
  988.8 5.7 add.411
  998.5 4.3 add.391
  1008.3 2.8 collective-permute-done.52
  1017.6 4.8 collective-permute-done.80
  1026.5 6.5 maximum_add_fusion
  1041.0 14.5 %collective-permute-done.68 = bf16[1,160,1024]{2,1,0:T(8,128)(2,1)S(1)} collective-permute-done((bf16[1,160,1024]{2,1,0:T(8,128)(2,1)S(1)}, bf16[1,160,1024]{2,1,0:T(8,128)(2,1)S(1)}, u32[]{:S(2)}, u32[]{:S(2)}) %collective-permute-start.68) | collective-permute-done | bytes 327712 | tf_op jit(solution)/shard_map/ppermute | solution.py:24
  1055.6 11.1 collective-permute-done.55
  1073.0 2.7 collective-permute-start.82
  1081.2 2.7 collective-permute-start.60
  1083.9 8.8 collective-permute-done.64
  1096.9 4.2 collective-permute-start.83
  1103.3 3.7 collective-permute-done.66
  1111.5 9.5 collective-permute-done.65
  1121.3 2.7 collective-permute-start.71
  1124.7 12.6 %collective-permute-done.71 = bf16[1,160,1024]{2,1,0:T(8,128)(2,1)S(1)} collective-permute-done((bf16[1,160,1024]{2,1,0:T(8,128)(2,1)S(1)}, bf16[1,160,1024]{2,1,0:T(8,128)(2,1)S(1)}, u32[]{:S(2)}, u32[]{:S(2)}) %collective-permute-start.71) | collective-permute-done | bytes 327712 | tf_op jit(solution)/shard_map/ppermute | solution.py:24
  1137.4 2.4 collective-permute-start.72
  (497 shorter events, 191.1 us)
Async XLA Ops:
  3.5 20.5 %collective-permute-start.1 = (bf16[1,128,1024]{2,1,0:T(8,128)(2,1)S(1)}, bf16[1,128,1024]{2,1,0:T(8,128)(2,1)S(1)}, u32[]{:S(2)}, u32[]{:S(2)}) collective-permute-start(bf16[1,128,1024]{2,1,0:T(8,128)(2,1)S(1)} %maximum_bitcast_fusion.1), channel_id=1, source_target_pairs={{0,8},{1,9},{2,10},{3,11},{4,12},{5,13},{6,14},{7,15},{8,0},{9,1},... | collective-permute-start | bytes 786440 | tf_op jit(solution)/shard_map/ppermute | solution.py:24
  8.4 36.2 %collective-permute-start.30 = (bf16[1,128,1024]{2,1,0:T(8,128)(2,1)S(1)}, bf16[1,128,1024]{2,1,0:T(8,128)(2,1)S(1)}, u32[]{:S(2)}, u32[]{:S(2)}) collective-permute-start(bf16[1,128,1024]{2,1,0:T(8,128)(2,1)S(1)} %get-tuple-element.171), channel_id=1, source_target_pairs={{0,8},{1,9},{2,10},{3,11},{4,12},{5,13},{6,14},{7,15},{8,0},{9,1},... | collective-permute-start | bytes 786440 | tf_op jit(solution)/shard_map/ppermute | solution.py:24
  24.8 16.8 %collective-permute-start.4 = (bf16[2,128,1024]{2,1,0:T(8,128)(2,1)}, bf16[2,128,1024]{2,1,0:T(8,128)(2,1)}, u32[]{:S(2)}, u32[]{:S(2)}) collective-permute-start(bf16[2,128,1024]{2,1,0:T(8,128)(2,1)} %pad_maximum_fusion.6), channel_id=1, source_target_pairs={{0,4},{1,5},{2,6},{3,7},{4,0},{5,1},{6,2},{7,3},{8,12},{9,13},{10,... | collective-permute-start | bytes 1572872 | tf_op jit(solution)/shard_map/ppermute | solution.py:24
  26.3 20.1 %collective-permute-start.2 = (bf16[2,128,1024]{2,1,0:T(8,128)(2,1)}, bf16[2,128,1024]{2,1,0:T(8,128)(2,1)}, u32[]{:S(2)}, u32[]{:S(2)}) collective-permute-start(bf16[2,128,1024]{2,1,0:T(8,128)(2,1)} %pad_maximum_fusion.6), channel_id=1, source_target_pairs={{0,1},{1,0},{2,3},{3,2},{4,5},{5,4},{6,7},{7,6},{8,9},{9,8},{10,11... | collective-permute-start | bytes 1572872 | tf_op jit(solution)/shard_map/ppermute | solution.py:24
  27.6 18.6 %collective-permute-start.3 = (bf16[2,128,1024]{2,1,0:T(8,128)(2,1)}, bf16[2,128,1024]{2,1,0:T(8,128)(2,1)}, u32[]{:S(2)}, u32[]{:S(2)}) collective-permute-start(bf16[2,128,1024]{2,1,0:T(8,128)(2,1)} %pad_maximum_fusion.6), channel_id=1, source_target_pairs={{0,2},{1,3},{2,0},{3,1},{4,6},{5,7},{6,4},{7,5},{8,10},{9,11},{10,... | collective-permute-start | bytes 1572872 | tf_op jit(solution)/shard_map/ppermute | solution.py:24
  41.6 13.2 %collective-permute-start.6 = (bf16[2,128,1024]{2,1,0:T(8,128)(2,1)}, bf16[2,128,1024]{2,1,0:T(8,128)(2,1)S(1)}, u32[]{:S(2)}, u32[]{:S(2)}) collective-permute-start(bf16[2,128,1024]{2,1,0:T(8,128)(2,1)} %collective-permute-done.4), channel_id=1, source_target_pairs={{0,2},{1,3},{2,0},{3,1},{4,6},{5,7},{6,4},{7,5},{8,10},{9,11},{10,... | collective-permute-start | bytes 1572872 | tf_op jit(solution)/shard_map/ppermute | solution.py:24
  44.7 25.9 %collective-permute-start.31 = (bf16[2,128,1024]{2,1,0:T(8,128)(2,1)S(1)}, bf16[2,128,1024]{2,1,0:T(8,128)(2,1)S(1)}, u32[]{:S(2)}, u32[]{:S(2)}) collective-permute-start(bf16[2,128,1024]{2,1,0:T(8,128)(2,1)S(1)} %pad_maximum_fusion.8), channel_id=1, source_target_pairs={{0,1},{1,0},{2,3},{3,2},{4,5},{5,4},{6,7},{7,6},{8,9},{9,8},{10,11... | collective-permute-start | bytes 1572872 | tf_op jit(solution)/shard_map/ppermute | solution.py:24
  46.0 27.2 %collective-permute-start.32 = (bf16[2,128,1024]{2,1,0:T(8,128)(2,1)S(1)}, bf16[2,128,1024]{2,1,0:T(8,128)(2,1)S(1)}, u32[]{:S(2)}, u32[]{:S(2)}) collective-permute-start(bf16[2,128,1024]{2,1,0:T(8,128)(2,1)S(1)} %pad_maximum_fusion.8), channel_id=1, source_target_pairs={{0,2},{1,3},{2,0},{3,1},{4,6},{5,7},{6,4},{7,5},{8,10},{9,11},{10,... | collective-permute-start | bytes 1572872 | tf_op jit(solution)/shard_map/ppermute | solution.py:24
  46.2 22.4 %collective-permute-start.5 = (bf16[2,128,1024]{2,1,0:T(8,128)(2,1)}, bf16[2,128,1024]{2,1,0:T(8,128)(2,1)S(1)}, u32[]{:S(2)}, u32[]{:S(2)}) collective-permute-start(bf16[2,128,1024]{2,1,0:T(8,128)(2,1)} %collective-permute-done.3), channel_id=1, source_target_pairs={{0,1},{1,0},{2,3},{3,2},{4,5},{5,4},{6,7},{7,6},{8,9},{9,8},{10,11... | collective-permute-start | bytes 1572872 | tf_op jit(solution)/shard_map/ppermute | solution.py:24
  46.5 14.1 %collective-permute-start.7 = (bf16[2,128,1024]{2,1,0:T(8,128)(2,1)}, bf16[2,128,1024]{2,1,0:T(8,128)(2,1)S(1)}, u32[]{:S(2)}, u32[]{:S(2)}) collective-permute-start(bf16[2,128,1024]{2,1,0:T(8,128)(2,1)} %collective-permute-done.2), channel_id=1, source_target_pairs={{0,4},{1,5},{2,6},{3,7},{4,0},{5,1},{6,2},{7,3},{8,12},{9,13},{10,... | collective-permute-start | bytes 1572872 | tf_op jit(solution)/shard_map/ppermute | solution.py:24
  54.9 17.1 %collective-permute-start.33 = (bf16[2,128,1024]{2,1,0:T(8,128)(2,1)S(1)}, bf16[2,128,1024]{2,1,0:T(8,128)(2,1)S(1)}, u32[]{:S(2)}, u32[]{:S(2)}) collective-permute-start(bf16[2,128,1024]{2,1,0:T(8,128)(2,1)S(1)} %pad_maximum_fusion.8), channel_id=1, source_target_pairs={{0,4},{1,5},{2,6},{3,7},{4,0},{5,1},{6,2},{7,3},{8,12},{9,13},{10,... | collective-permute-start | bytes 1572872 | tf_op jit(solution)/shard_map/ppermute | solution.py:24
  60.5 15.7 %collective-permute-start.8 = (bf16[1,128,1024]{2,1,0:T(8,128)(2,1)S(1)}, bf16[1,128,1024]{2,1,0:T(8,128)(2,1)S(1)}, u32[]{:S(2)}, u32[]{:S(2)}) collective-permute-start(bf16[1,128,1024]{2,1,0:T(8,128)(2,1)S(1)} %slice.441), channel_id=1, source_target_pairs={{0,1},{1,0},{2,3},{3,2},{4,5},{5,4},{6,7},{7,6},{8,9},{9,8},{10,11... | collective-permute-start | bytes 786440 | tf_op jit(solution)/shard_map/ppermute | solution.py:24
  68.6 9.6 collective-permute-start.9
  70.6 16.6 %collective-permute-start.20 = (bf16[1,160,1024]{2,1,0:T(8,128)(2,1)S(1)}, bf16[1,160,1024]{2,1,0:T(8,128)(2,1)S(1)}, u32[]{:S(2)}, u32[]{:S(2)}) collective-permute-start(bf16[1,160,1024]{2,1,0:T(8,128)(2,1)S(1)} %maximum_bitcast_fusion), channel_id=1, source_target_pairs={{0,8},{1,9},{2,10},{3,11},{4,12},{5,13},{6,14},{7,15},{8,0},{9,1},... | collective-permute-start | bytes 983048 | tf_op jit(solution)/shard_map/ppermute | solution.py:24
  72.0 17.6 %collective-permute-start.35 = (bf16[2,128,1024]{2,1,0:T(8,128)(2,1)S(1)}, bf16[2,128,1024]{2,1,0:T(8,128)(2,1)S(1)}, u32[]{:S(2)}, u32[]{:S(2)}) collective-permute-start(bf16[2,128,1024]{2,1,0:T(8,128)(2,1)S(1)} %collective-permute-done.33), channel_id=1, source_target_pairs={{0,2},{1,3},{2,0},{3,1},{4,6},{5,7},{6,4},{7,5},{8,10},{9,11},{10,... | collective-permute-start | bytes 1572872 | tf_op jit(solution)/shard_map/ppermute | solution.py:24
  73.2 17.6 %collective-permute-start.36 = (bf16[2,128,1024]{2,1,0:T(8,128)(2,1)S(1)}, bf16[2,128,1024]{2,1,0:T(8,128)(2,1)S(1)}, u32[]{:S(2)}, u32[]{:S(2)}) collective-permute-start(bf16[2,128,1024]{2,1,0:T(8,128)(2,1)S(1)} %collective-permute-done.31), channel_id=1, source_target_pairs={{0,4},{1,5},{2,6},{3,7},{4,0},{5,1},{6,2},{7,3},{8,12},{9,13},{10,... | collective-permute-start | bytes 1572872 | tf_op jit(solution)/shard_map/ppermute | solution.py:24
  76.2 16.9 %collective-permute-start.34 = (bf16[2,128,1024]{2,1,0:T(8,128)(2,1)S(1)}, bf16[2,128,1024]{2,1,0:T(8,128)(2,1)S(1)}, u32[]{:S(2)}, u32[]{:S(2)}) collective-permute-start(bf16[2,128,1024]{2,1,0:T(8,128)(2,1)S(1)} %collective-permute-done.32), channel_id=1, source_target_pairs={{0,1},{1,0},{2,3},{3,2},{4,5},{5,4},{6,7},{7,6},{8,9},{9,8},{10,11... | collective-permute-start | bytes 1572872 | tf_op jit(solution)/shard_map/ppermute | solution.py:24
  78.9 76.2 %collective-permute-start.10 = (bf16[16,128,1024]{2,1,0:T(8,128)(2,1)}, bf16[16,128,1024]{2,1,0:T(8,128)(2,1)}, u32[]{:S(2)}, u32[]{:S(2)}) collective-permute-start(bf16[16,128,1024]{2,1,0:T(8,128)(2,1)} %constant_dynamic-update-slice_fusion.own_ref), channel_id=1, source_target_pairs={{0,16},{16,0},{1,17},{17,1},{2,18},{18,2},{3,19},{19,3},{4,20},{20... | collective-permute-start | bytes 12582920 | tf_op jit(solution)/shard_map/ppermute | solution.py:29
  87.3 15.0 %collective-permute-start.21 = (bf16[2,160,1024]{2,1,0:T(8,128)(2,1)S(1)}, bf16[2,160,1024]{2,1,0:T(8,128)(2,1)S(1)}, u32[]{:S(2)}, u32[]{:S(2)}) collective-permute-start(bf16[2,160,1024]{2,1,0:T(8,128)(2,1)S(1)} %pad_maximum_fusion.2), channel_id=1, source_target_pairs={{0,1},{1,0},{2,3},{3,2},{4,5},{5,4},{6,7},{7,6},{8,9},{9,8},{10,11... | collective-permute-start | bytes 1966088 | tf_op jit(solution)/shard_map/ppermute | solution.py:24
  89.5 14.6 %collective-permute-start.22 = (bf16[2,160,1024]{2,1,0:T(8,128)(2,1)S(1)}, bf16[2,160,1024]{2,1,0:T(8,128)(2,1)S(1)}, u32[]{:S(2)}, u32[]{:S(2)}) collective-permute-start(bf16[2,160,1024]{2,1,0:T(8,128)(2,1)S(1)} %pad_maximum_fusion.2), channel_id=1, source_target_pairs={{0,2},{1,3},{2,0},{3,1},{4,6},{5,7},{6,4},{7,5},{8,10},{9,11},{10,... | collective-permute-start | bytes 1966088 | tf_op jit(solution)/shard_map/ppermute | solution.py:24
  90.8 14.6 %collective-permute-start.23 = (bf16[2,160,1024]{2,1,0:T(8,128)(2,1)S(1)}, bf16[2,160,1024]{2,1,0:T(8,128)(2,1)S(1)}, u32[]{:S(2)}, u32[]{:S(2)}) collective-permute-start(bf16[2,160,1024]{2,1,0:T(8,128)(2,1)S(1)} %pad_maximum_fusion.2), channel_id=1, source_target_pairs={{0,4},{1,5},{2,6},{3,7},{4,0},{5,1},{6,2},{7,3},{8,12},{9,13},{10,... | collective-permute-start | bytes 1966088 | tf_op jit(solution)/shard_map/ppermute | solution.py:24
  93.1 14.8 %collective-permute-start.37 = (bf16[1,128,1024]{2,1,0:T(8,128)(2,1)S(1)}, bf16[1,128,1024]{2,1,0:T(8,128)(2,1)S(1)}, u32[]{:S(2)}, u32[]{:S(2)}) collective-permute-start(bf16[1,128,1024]{2,1,0:T(8,128)(2,1)S(1)} %slice.456), channel_id=1, source_target_pairs={{0,1},{1,0},{2,3},{3,2},{4,5},{5,4},{6,7},{7,6},{8,9},{9,8},{10,11... | collective-permute-start | bytes 786440 | tf_op jit(solution)/shard_map/ppermute | solution.py:24
  104.2 23.0 %collective-permute-start.24 = (bf16[2,160,1024]{2,1,0:T(8,128)(2,1)S(1)}, bf16[2,160,1024]{2,1,0:T(8,128)(2,1)S(1)}, u32[]{:S(2)}, u32[]{:S(2)}) collective-permute-start(bf16[2,160,1024]{2,1,0:T(8,128)(2,1)S(1)} %collective-permute-done.22), channel_id=1, source_target_pairs={{0,1},{1,0},{2,3},{3,2},{4,5},{5,4},{6,7},{7,6},{8,9},{9,8},{10,11... | collective-permute-start | bytes 1966088 | tf_op jit(solution)/shard_map/ppermute | solution.py:24
  105.4 17.0 %collective-permute-start.25 = (bf16[2,160,1024]{2,1,0:T(8,128)(2,1)S(1)}, bf16[2,160,1024]{2,1,0:T(8,128)(2,1)S(1)}, u32[]{:S(2)}, u32[]{:S(2)}) collective-permute-start(bf16[2,160,1024]{2,1,0:T(8,128)(2,1)S(1)} %collective-permute-done.23), channel_id=1, source_target_pairs={{0,2},{1,3},{2,0},{3,1},{4,6},{5,7},{6,4},{7,5},{8,10},{9,11},{10,... | collective-permute-start | bytes 1966088 | tf_op jit(solution)/shard_map/ppermute | solution.py:24
  107.9 16.4 %collective-permute-start.26 = (bf16[2,160,1024]{2,1,0:T(8,128)(2,1)S(1)}, bf16[2,160,1024]{2,1,0:T(8,128)(2,1)S(1)}, u32[]{:S(2)}, u32[]{:S(2)}) collective-permute-start(bf16[2,160,1024]{2,1,0:T(8,128)(2,1)S(1)} %collective-permute-done.21), channel_id=1, source_target_pairs={{0,4},{1,5},{2,6},{3,7},{4,0},{5,1},{6,2},{7,3},{8,12},{9,13},{10,... | collective-permute-start | bytes 1966088 | tf_op jit(solution)/shard_map/ppermute | solution.py:24
  110.3 309.6 %collective-permute-start.39 = (bf16[16,128,1024]{2,1,0:T(8,128)(2,1)}, bf16[16,128,1024]{2,1,0:T(8,128)(2,1)}, u32[]{:S(2)}, u32[]{:S(2)}) collective-permute-start(bf16[16,128,1024]{2,1,0:T(8,128)(2,1)} %get-tuple-element.236), channel_id=1, source_target_pairs={{0,16},{16,0},{1,17},{17,1},{2,18},{18,2},{3,19},{19,3},{4,20},{20... | collective-permute-start | bytes 12582920 | tf_op jit(solution)/shard_map/ppermute | solution.py:29
  122.4 20.3 %collective-permute-start = (bf16[1,1024]{1,0:T(2,128)(2,1)S(1)}, bf16[1,1024]{1,0:T(2,128)(2,1)S(1)}, u32[]{:S(2)}, u32[]{:S(2)}) collective-permute-start(bf16[1,1024]{1,0:T(2,128)(2,1)S(1)} %slice.337), channel_id=1, source_target_pairs={{0,1},{1,2},{2,3},{3,4},{4,5},{5,6},{6,7},{7,8},{8,9},{9,10},{10,1... | collective-permute-start | bytes 6152 | tf_op jit(solution)/shard_map/ppermute | solution.py:438
  131.6 8.5 collective-permute-start.11
  134.6 313.5 %collective-permute-start.29 = (bf16[16,160,1024]{2,1,0:T(8,128)(2,1)}, bf16[16,160,1024]{2,1,0:T(8,128)(2,1)}, u32[]{:S(2)}, u32[]{:S(2)}) collective-permute-start(bf16[16,160,1024]{2,1,0:T(8,128)(2,1)} %constant_dynamic-update-slice_fusion.20.own_ref), channel_id=1, source_target_pairs={{0,16},{16,0},{1,17},{17,1},{2,18},{18,2},{3,19},{19,3},{4,20},{20... | collective-permute-start | bytes 15728648 | tf_op jit(solution)/shard_map/ppermute | solution.py:29
  444.4 81.6 %collective-permute-start.19 = (bf16[1,1024]{1,0:T(2,128)(2,1)S(1)}, bf16[1,1024]{1,0:T(2,128)(2,1)S(1)}, u32[]{:S(2)}, u32[]{:S(2)}) collective-permute-start(bf16[1,1024]{1,0:T(2,128)(2,1)S(1)} %slice.450), channel_id=1, source_target_pairs={{0,1},{1,2},{2,3},{3,4},{4,5},{5,6},{6,7},{7,8},{8,9},{9,10},{10,1... | collective-permute-start | bytes 6152 | tf_op jit(solution)/shard_map/ppermute | solution.py:479
  565.3 86.0 %collective-permute-start.40 = (f32[1,1024]{1,0:T(1,128)S(1)}, f32[1,1024]{1,0:T(1,128)S(1)}, u32[]{:S(2)}, u32[]{:S(2)}) collective-permute-start(f32[1,1024]{1,0:T(1,128)S(1)} %slice.459), channel_id=1, source_target_pairs={{1,0},{2,1},{3,2},{4,3},{5,4},{6,5},{7,6},{8,7},{9,8},{10,9},{11,1... | collective-permute-start | bytes 12296 | tf_op jit(solution)/shard_map/ppermute | solution.py:519
  570.3 418.4 %collective-permute-start.73 = (bf16[16,128,1024]{2,1,0:T(8,128)(2,1)}, bf16[16,128,1024]{2,1,0:T(8,128)(2,1)}, u32[]{:S(2)}, u32[]{:S(2)}) collective-permute-start(bf16[16,128,1024]{2,1,0:T(8,128)(2,1)} %bitcast.79), channel_id=1, source_target_pairs={{0,16},{16,0},{1,17},{17,1},{2,18},{18,2},{3,19},{19,3},{4,20},{20... | collective-permute-start | bytes 12582920 | tf_op jit(solution)/shard_map/ppermute | solution.py:29
  944.8 52.8 %collective-permute-start.51 = (bf16[16,128,1024]{2,1,0:T(8,128)(2,1)}, bf16[16,128,1024]{2,1,0:T(8,128)(2,1)}, u32[]{:S(2)}, u32[]{:S(2)}) collective-permute-start(bf16[16,128,1024]{2,1,0:T(8,128)(2,1)} %get-tuple-element.47), channel_id=1, source_target_pairs={{0,16},{16,0},{1,17},{17,1},{2,18},{18,2},{3,19},{19,3},{4,20},{20... | collective-permute-start | bytes 12582920 | tf_op jit(solution)/shard_map/ppermute | solution.py:29
  958.4 68.0 %collective-permute-start.62 = (bf16[16,160,1024]{2,1,0:T(8,128)(2,1)}, bf16[16,160,1024]{2,1,0:T(8,128)(2,1)}, u32[]{:S(2)}, u32[]{:S(2)}) collective-permute-start(bf16[16,160,1024]{2,1,0:T(8,128)(2,1)} %pad_maximum_fusion.1), channel_id=1, source_target_pairs={{0,16},{16,0},{1,17},{17,1},{2,18},{18,2},{3,19},{19,3},{4,20},{20... | collective-permute-start | bytes 15728648 | tf_op jit(solution)/shard_map/ppermute | solution.py:29
  982.7 14.8 %collective-permute-start.50 = (f32[11,1024]{1,0:T(8,128)S(1)}, f32[11,1024]{1,0:T(8,128)S(1)}, u32[]{:S(2)}, u32[]{:S(2)}) collective-permute-start(f32[11,1024]{1,0:T(8,128)S(1)} %add.388), channel_id=1, source_target_pairs={{0,16},{16,0},{1,17},{17,1},{2,18},{18,2},{3,19},{19,3},{4,20},{20... | collective-permute-start | bytes 135176 | tf_op jit(solution)/shard_map/ppermute | solution.py:83
  994.5 10.0 collective-permute-start.74
  994.6 10.0 collective-permute-start.79
  1002.9 8.2 collective-permute-start.52
  1003.0 8.1 collective-permute-start.57
  1004.7 12.9 %collective-permute-start.75 = (bf16[2,128,1024]{2,1,0:T(8,128)(2,1)S(1)}, bf16[2,128,1024]{2,1,0:T(8,128)(2,1)S(1)}, u32[]{:S(2)}, u32[]{:S(2)}) collective-permute-start(bf16[2,128,1024]{2,1,0:T(8,128)(2,1)S(1)} %pad_maximum_fusion.11), channel_id=1, source_target_pairs={{0,4},{1,5},{2,6},{3,7},{4,0},{5,1},{6,2},{7,3},{8,12},{9,13},{10,... | collective-permute-start | bytes 1572872 | tf_op jit(solution)/shard_map/ppermute | solution.py:24
  1006.2 16.2 %collective-permute-start.80 = (bf16[2,128,1024]{2,1,0:T(8,128)(2,1)S(1)}, bf16[2,128,1024]{2,1,0:T(8,128)(2,1)S(1)}, u32[]{:S(2)}, u32[]{:S(2)}) collective-permute-start(bf16[2,128,1024]{2,1,0:T(8,128)(2,1)S(1)} %pad_maximum_fusion.12), channel_id=1, source_target_pairs={{0,2},{1,3},{2,0},{3,1},{4,6},{5,7},{6,4},{7,5},{8,10},{9,11},{10,... | collective-permute-start | bytes 1572872 | tf_op jit(solution)/shard_map/ppermute | solution.py:24
  1012.0 21.1 %collective-permute-start.53 = (bf16[2,128,1024]{2,1,0:T(8,128)(2,1)}, bf16[2,128,1024]{2,1,0:T(8,128)(2,1)}, u32[]{:S(2)}, u32[]{:S(2)}) collective-permute-start(bf16[2,128,1024]{2,1,0:T(8,128)(2,1)} %pad_maximum_fusion.9), channel_id=1, source_target_pairs={{0,4},{1,5},{2,6},{3,7},{4,0},{5,1},{6,2},{7,3},{8,12},{9,13},{10,... | collective-permute-start | bytes 1572872 | tf_op jit(solution)/shard_map/ppermute | solution.py:24
  1014.2 19.5 %collective-permute-start.58 = (bf16[2,128,1024]{2,1,0:T(8,128)(2,1)}, bf16[2,128,1024]{2,1,0:T(8,128)(2,1)}, u32[]{:S(2)}, u32[]{:S(2)}) collective-permute-start(bf16[2,128,1024]{2,1,0:T(8,128)(2,1)} %pad_maximum_fusion.10), channel_id=1, source_target_pairs={{0,2},{1,3},{2,0},{3,1},{4,6},{5,7},{6,4},{7,5},{8,10},{9,11},{10,... | collective-permute-start | bytes 1572872 | tf_op jit(solution)/shard_map/ppermute | solution.py:24
  1023.7 45.5 %collective-permute-start.81 = (bf16[2,128,1024]{2,1,0:T(8,128)(2,1)}, bf16[2,128,1024]{2,1,0:T(8,128)(2,1)}, u32[]{:S(2)}, u32[]{:S(2)}) collective-permute-start(bf16[2,128,1024]{2,1,0:T(8,128)(2,1)} %get-tuple-element.188), channel_id=1, source_target_pairs={{0,4},{1,5},{2,6},{3,7},{4,0},{5,1},{6,2},{7,3},{8,12},{9,13},{10,... | collective-permute-start | bytes 1572872 | tf_op jit(solution)/shard_map/ppermute | solution.py:24
  1025.1 12.3 %collective-permute-start.77 = (bf16[2,128,1024]{2,1,0:T(8,128)(2,1)}, bf16[2,128,1024]{2,1,0:T(8,128)(2,1)}, u32[]{:S(2)}, u32[]{:S(2)}) collective-permute-start(bf16[2,128,1024]{2,1,0:T(8,128)(2,1)} %get-tuple-element.189), channel_id=1, source_target_pairs={{0,1},{1,0},{2,3},{3,2},{4,5},{5,4},{6,7},{7,6},{8,9},{9,8},{10,11... | collective-permute-start | bytes 1572872 | tf_op jit(solution)/shard_map/ppermute | solution.py:24
  1026.4 43.8 %collective-permute-start.76 = (bf16[2,128,1024]{2,1,0:T(8,128)(2,1)}, bf16[2,128,1024]{2,1,0:T(8,128)(2,1)}, u32[]{:S(2)}, u32[]{:S(2)}) collective-permute-start(bf16[2,128,1024]{2,1,0:T(8,128)(2,1)} %get-tuple-element.187), channel_id=1, source_target_pairs={{0,1},{1,0},{2,3},{3,2},{4,5},{5,4},{6,7},{7,6},{8,9},{9,8},{10,11... | collective-permute-start | bytes 1572872 | tf_op jit(solution)/shard_map/ppermute | solution.py:24
  1033.2 7.4 collective-permute-start.63
  1033.7 21.8 %collective-permute-start.68 = (bf16[1,160,1024]{2,1,0:T(8,128)(2,1)S(1)}, bf16[1,160,1024]{2,1,0:T(8,128)(2,1)S(1)}, u32[]{:S(2)}, u32[]{:S(2)}) collective-permute-start(bf16[1,160,1024]{2,1,0:T(8,128)(2,1)S(1)} %get-tuple-element.183), channel_id=1, source_target_pairs={{0,1},{1,0},{2,3},{3,2},{4,5},{5,4},{6,7},{7,6},{8,9},{9,8},{10,11... | collective-permute-start | bytes 983048 | tf_op jit(solution)/shard_map/ppermute | solution.py:24
  1037.3 29.4 %collective-permute-start.55 = (bf16[2,128,1024]{2,1,0:T(8,128)(2,1)S(1)}, bf16[2,128,1024]{2,1,0:T(8,128)(2,1)S(1)}, u32[]{:S(2)}, u32[]{:S(2)}) collective-permute-start(bf16[2,128,1024]{2,1,0:T(8,128)(2,1)S(1)} %get-tuple-element.198), channel_id=1, source_target_pairs={{0,1},{1,0},{2,3},{3,2},{4,5},{5,4},{6,7},{7,6},{8,9},{9,8},{10,11... | collective-permute-start | bytes 1572872 | tf_op jit(solution)/shard_map/ppermute | solution.py:24
  1040.5 32.4 %collective-permute-start.59 = (bf16[2,128,1024]{2,1,0:T(8,128)(2,1)S(1)}, bf16[2,128,1024]{2,1,0:T(8,128)(2,1)S(1)}, u32[]{:S(2)}, u32[]{:S(2)}) collective-permute-start(bf16[2,128,1024]{2,1,0:T(8,128)(2,1)S(1)} %get-tuple-element.197), channel_id=1, source_target_pairs={{0,4},{1,5},{2,6},{3,7},{4,0},{5,1},{6,2},{7,3},{8,12},{9,13},{10,... | collective-permute-start | bytes 1572872 | tf_op jit(solution)/shard_map/ppermute | solution.py:24
  1055.5 14.7 %collective-permute-start.78 = (bf16[2,128,1024]{2,1,0:T(8,128)(2,1)S(1)}, bf16[2,128,1024]{2,1,0:T(8,128)(2,1)S(1)}, u32[]{:S(2)}, u32[]{:S(2)}) collective-permute-start(bf16[2,128,1024]{2,1,0:T(8,128)(2,1)S(1)} %slice_add_fusion.5), channel_id=1, source_target_pairs={{0,2},{1,3},{2,0},{3,1},{4,6},{5,7},{6,4},{7,5},{8,10},{9,11},{10,... | collective-permute-start | bytes 1572872 | tf_op jit(solution)/shard_map/ppermute | solution.py:24
  1066.7 11.0 collective-permute-start.54
  1069.2 10.9 collective-permute-start.56
  1070.1 22.6 %collective-permute-start.64 = (bf16[2,160,1024]{2,1,0:T(8,128)(2,1)S(1)}, bf16[2,160,1024]{2,1,0:T(8,128)(2,1)S(1)}, u32[]{:S(2)}, u32[]{:S(2)}) collective-permute-start(bf16[2,160,1024]{2,1,0:T(8,128)(2,1)S(1)} %pad_maximum_fusion.3), channel_id=1, source_target_pairs={{0,4},{1,5},{2,6},{3,7},{4,0},{5,1},{6,2},{7,3},{8,12},{9,13},{10,... | collective-permute-start | bytes 1966088 | tf_op jit(solution)/shard_map/ppermute | solution.py:24
  1070.2 23.9 %collective-permute-start.69 = (bf16[2,160,1024]{2,1,0:T(8,128)(2,1)S(1)}, bf16[2,160,1024]{2,1,0:T(8,128)(2,1)S(1)}, u32[]{:S(2)}, u32[]{:S(2)}) collective-permute-start(bf16[2,160,1024]{2,1,0:T(8,128)(2,1)S(1)} %pad_maximum_fusion.4), channel_id=1, source_target_pairs={{0,2},{1,3},{2,0},{3,1},{4,6},{5,7},{6,4},{7,5},{8,10},{9,11},{10,... | collective-permute-start | bytes 1966088 | tf_op jit(solution)/shard_map/ppermute | solution.py:24
  1073.0 23.9 %collective-permute-start.82 = (bf16[1,128,1024]{2,1,0:T(8,128)(2,1)S(1)}, bf16[1,128,1024]{2,1,0:T(8,128)(2,1)S(1)}, u32[]{:S(2)}, u32[]{:S(2)}) collective-permute-start(bf16[1,128,1024]{2,1,0:T(8,128)(2,1)S(1)} %slice.530), channel_id=1, source_target_pairs={{0,8},{1,9},{2,10},{3,11},{4,12},{5,13},{6,14},{7,15},{8,0},{9,1},... | collective-permute-start | bytes 786440 | tf_op jit(solution)/shard_map/ppermute | solution.py:24
  1081.2 19.8 %collective-permute-start.60 = (bf16[1,128,1024]{2,1,0:T(8,128)(2,1)S(1)}, bf16[1,128,1024]{2,1,0:T(8,128)(2,1)S(1)}, u32[]{:S(2)}, u32[]{:S(2)}) collective-permute-start(bf16[1,128,1024]{2,1,0:T(8,128)(2,1)S(1)} %slice.490), channel_id=1, source_target_pairs={{0,8},{1,9},{2,10},{3,11},{4,12},{5,13},{6,14},{7,15},{8,0},{9,1},... | collective-permute-start | bytes 786440 | tf_op jit(solution)/shard_map/ppermute | solution.py:24
  1094.3 12.8 %collective-permute-start.66 = (bf16[2,160,1024]{2,1,0:T(8,128)(2,1)S(1)}, bf16[2,160,1024]{2,1,0:T(8,128)(2,1)S(1)}, u32[]{:S(2)}, u32[]{:S(2)}) collective-permute-start(bf16[2,160,1024]{2,1,0:T(8,128)(2,1)S(1)} %get-tuple-element.180), channel_id=1, source_target_pairs={{0,1},{1,0},{2,3},{3,2},{4,5},{5,4},{6,7},{7,6},{8,9},{9,8},{10,11... | collective-permute-start | bytes 1966088 | tf_op jit(solution)/shard_map/ppermute | solution.py:24
  1094.9 16.6 %collective-permute-start.70 = (bf16[2,160,1024]{2,1,0:T(8,128)(2,1)S(1)}, bf16[2,160,1024]{2,1,0:T(8,128)(2,1)S(1)}, u32[]{:S(2)}, u32[]{:S(2)}) collective-permute-start(bf16[2,160,1024]{2,1,0:T(8,128)(2,1)S(1)} %get-tuple-element.179), channel_id=1, source_target_pairs={{0,4},{1,5},{2,6},{3,7},{4,0},{5,1},{6,2},{7,3},{8,12},{9,13},{10,... | collective-permute-start | bytes 1966088 | tf_op jit(solution)/shard_map/ppermute | solution.py:24
  1095.7 25.3 %collective-permute-start.65 = (bf16[2,160,1024]{2,1,0:T(8,128)(2,1)S(1)}, bf16[2,160,1024]{2,1,0:T(8,128)(2,1)S(1)}, u32[]{:S(2)}, u32[]{:S(2)}) collective-permute-start(bf16[2,160,1024]{2,1,0:T(8,128)(2,1)S(1)} %get-tuple-element.178), channel_id=1, source_target_pairs={{0,1},{1,0},{2,3},{3,2},{4,5},{5,4},{6,7},{7,6},{8,9},{9,8},{10,11... | collective-permute-start | bytes 1966088 | tf_op jit(solution)/shard_map/ppermute | solution.py:24
  1096.9 12.1 %collective-permute-start.83 = (bf16[128,1024]{1,0:T(8,128)(2,1)S(1)}, bf16[128,1024]{1,0:T(8,128)(2,1)S(1)}, u32[]{:S(2)}, u32[]{:S(2)}) collective-permute-start(bf16[128,1024]{1,0:T(8,128)(2,1)S(1)} %fusion.43), channel_id=1, source_target_pairs={{0,16},{16,0},{1,17},{17,1},{2,18},{18,2},{3,19},{19,3},{4,20},{20... | collective-permute-start | bytes 786440 | tf_op jit(solution)/shard_map/ppermute | solution.py:29
  1101.1 9.0 collective-permute-start.61
  1107.1 14.0 %collective-permute-start.67 = (bf16[2,160,1024]{2,1,0:T(8,128)(2,1)S(1)}, bf16[2,160,1024]{2,1,0:T(8,128)(2,1)S(1)}, u32[]{:S(2)}, u32[]{:S(2)}) collective-permute-start(bf16[2,160,1024]{2,1,0:T(8,128)(2,1)S(1)} %slice_add_fusion.1), channel_id=1, source_target_pairs={{0,2},{1,3},{2,0},{3,1},{4,6},{5,7},{6,4},{7,5},{8,10},{9,11},{10,... | collective-permute-start | bytes 1966088 | tf_op jit(solution)/shard_map/ppermute | solution.py:24
  1121.3 16.1 %collective-permute-start.71 = (bf16[1,160,1024]{2,1,0:T(8,128)(2,1)S(1)}, bf16[1,160,1024]{2,1,0:T(8,128)(2,1)S(1)}, u32[]{:S(2)}, u32[]{:S(2)}) collective-permute-start(bf16[1,160,1024]{2,1,0:T(8,128)(2,1)S(1)} %slice.513), channel_id=1, source_target_pairs={{0,8},{1,9},{2,10},{3,11},{4,12},{5,13},{6,14},{7,15},{8,0},{9,1},... | collective-permute-start | bytes 983048 | tf_op jit(solution)/shard_map/ppermute | solution.py:24
  (82 other events, 1013.2 us)

commit v2 on v1

--- a/solution.py
+++ b/solution.py
@@ -38,34 +38,80 @@
     return [k ^ i for k in (0, x, y, z, x ^ y, y ^ z, x ^ z, x ^ y ^ z) for i in low]
 
 
-def gather_chunk(part):
-    pre, (a, b, c) = bits_of(lax.axis_size("mp"))
-    v = part[None]
-    for bit in pre:
-        v = jnp.concatenate([v, swap(v, bit)], 0)
-    vx, vy, vz = swap(v, a), swap(v, b), swap(v, c)
-    xy, yz, xz = swap(vy, a), swap(vz, b), swap(vx, c)
-    half = v.shape[0] // 2
-    one, two = swap(yz[:half], a), swap(xz[half:], b)
-    return jnp.concatenate([v, vx, vy, vz, xy, yz, xz, one, two], 0)
-
-
-def scatter_chunk(part):
-    count = lax.axis_size("mp")
-    pre, (a, b, c) = bits_of(count)
-    p = part.reshape((8, count // 8) + part.shape[1:])
-    half = p.shape[1] // 2
-    one, two = swap(p[7, :half], a), swap(p[7, half:], b)
-    yz = jnp.concatenate([p[5, :half] + one, p[5, half:]], 0)
-    xz = jnp.concatenate([p[6, :half], p[6, half:] + two], 0)
-    y = p[2] + swap(p[4], a)
-    z = p[3] + swap(yz, b)
-    x = p[1] + swap(xz, c)
-    v = p[0] + swap(x, a) + swap(y, b) + swap(z, c)
-    for bit in reversed(pre):
-        half = v.shape[0] // 2
-        v = v[:half] + swap(v[half:], bit)
-    return v[0]
+def after(value, *earlier):
+    return lax.optimization_barrier((value,) + earlier)[0]
+
+
+class Gather:
+    def __init__(self, part):
+        self.v = part[None]
+
+    def wide(self, *earlier):
+        pre, _ = bits_of(lax.axis_size("mp"))
+        v = after(self.v, *earlier) if earlier else self.v
+        for bit in pre:
+            far = swap(v, bit)
+            v = jnp.concatenate([v, far], 0)
+        self.v, self.seen = v, (far,)
+
+    def near(self, *earlier):
+        _, (a, b, c) = bits_of(lax.axis_size("mp"))
+        v = after(self.v, *earlier) if earlier else self.v
+        self.first = self.seen = (swap(v, a), swap(v, b), swap(v, c))
+
+    def edge(self, *earlier):
+        _, (a, b, c) = bits_of(lax.axis_size("mp"))
+        x, y, z = self.first
+        self.second = self.seen = (swap(y, a), swap(z, b), swap(x, c))
+
+    def corner(self, *earlier):
+        _, (a, b, c) = bits_of(lax.axis_size("mp"))
+        _, yz, xz = self.second
+        half = yz.shape[0] // 2
+        self.third = self.seen = (swap(yz[:half], a), swap(xz[half:], b))
+        self.own = jnp.concatenate((self.v,) + self.first + self.second + self.third, 0)
+
+    def core(self):
+        self.other = swap_core(self.own)
+
+
+class Scatter:
+    def __init__(self, own, other):
+        self.own, self.far = own, swap_core(other)
+        self.seen = (self.far,)
+
+    def corner(self):
+        count = lax.axis_size("mp")
+        _, (a, b, c) = bits_of(count)
+        part = self.own + self.far
+        self.p = part.reshape((8, count // 8) + part.shape[1:])
+        half = self.p.shape[1] // 2
+        self.seen = (swap(self.p[7, :half], a), swap(self.p[7, half:], b))
+
+    def edge(self):
+        _, (a, b, c) = bits_of(lax.axis_size("mp"))
+        p = self.p
+        half = p.shape[1] // 2
+        one, two = self.seen
+        yz = jnp.concatenate([p[5, :half] + one, p[5, half:]], 0)
+        xz = jnp.concatenate([p[6, :half], p[6, half:] + two], 0)
+        self.seen = (swap(p[4], a), swap(yz, b), swap(xz, c))
+
+    def near(self):
+        _, (a, b, c) = bits_of(lax.axis_size("mp"))
+        p = self.p
+        y, z, x = p[2] + self.seen[0], p[3] + self.seen[1], p[1] + self.seen[2]
+        self.seen = (swap(x, a), swap(y, b), swap(z, c))
+
+    def wide(self):
+        pre, _ = bits_of(lax.axis_size("mp"))
+        v = self.p[0] + self.seen[0] + self.seen[1] + self.seen[2]
+        for bit in reversed(pre):
+            half = v.shape[0] // 2
+            far = swap(v[half:], bit)
+            v = v[:half] + far
+        self.seen = (far,)
+        self.sum = v[0]
 
 
 def gather_small(value):
@@ -86,6 +132,12 @@
 
 ANY = pl.BlockSpec(memory_space=pl.ANY)
 SMEM = pl.BlockSpec(memory_space=pltpu.SMEM)
+
+
+def cost(microseconds):
+    return pl.CostEstimate(
+        flops=0, bytes_accessed=int(microseconds * 3_000_000), transcendentals=0
+    )
 
 
 def place_kernel(pieces, count, places_ref, own_ref, other_ref, *rest):
@@ -116,8 +168,10 @@
             jax.ShapeDtypeStruct((2 * count * rows, width), own.dtype) for _, rows in pieces
         ),
         in_specs=[SMEM, ANY, ANY],
-        out_specs=tuple(ANY for _ in pieces),
+        out_specs=tuple(pl.BlockSpec(memory_space=pltpu.VMEM) for _ in pieces),
         scratch_shapes=[pltpu.SemaphoreType.DMA((2 * count * len(pieces),))],
+        compiler_params=pltpu.CompilerParams(vmem_limit_bytes=40 * 2**20),
+        cost_estimate=cost(4.0 * len(pieces)),
     )(places, own, other)
 
 
@@ -148,9 +202,11 @@
     return pl.pallas_call(
         functools.partial(unplace_kernel, pieces, count),
         out_shape=(shape, shape),
-        in_specs=[SMEM] + [ANY] * len(matrices),
+        in_specs=[SMEM] + [pl.BlockSpec(memory_space=pltpu.VMEM)] * len(matrices),
         out_specs=(ANY, ANY),
         scratch_shapes=[pltpu.SemaphoreType.DMA((2 * count * len(pieces),))],
+        compiler_params=pltpu.CompilerParams(vmem_limit_bytes=40 * 2**20),
+        cost_estimate=cost(4.0 * len(pieces)),
     )(places, *matrices)
 
 
@@ -303,6 +359,7 @@
         in_specs=[pl.BlockSpec(memory_space=pltpu.VMEM)] * len(args),
         out_specs=jax.tree.map(lambda _: pl.BlockSpec(memory_space=pltpu.VMEM), outs),
         compiler_params=pltpu.CompilerParams(vmem_limit_bytes=40 * 2**20),
+        cost_estimate=cost(4.0),
     )(*args)
 
 
@@ -390,10 +447,24 @@
     )
     chunk_b = jnp.concatenate([half_cols(hidden_key, hu), half_cols(hidden_recept, hc)], 0)
     chunk_c = half_rows(hidden_value, hu)
-    own_a = gather_chunk(chunk_a)
-    own_b = gather_chunk(chunk_b)
-    own_c = gather_chunk(chunk_c)
-    other_a, other_b, other_c = swap_core(own_a), swap_core(own_b), swap_core(own_c)
+    ga, gb, gc = Gather(chunk_a), Gather(chunk_b), Gather(chunk_c)
+    ga.wide()
+    ga.near()
+    gb.wide(*ga.seen[:0])
+    ga.edge()
+    gb.near(*ga.first)
+    ga.corner()
+    ga.core()
+    gc.wide(*gb.seen[:0])
+    gb.edge()
+    gc.near(*gb.first)
+    gb.corner()
+    gb.core()
+    gc.edge()
+    gc.corner()
+    gc.core()
+    own_a, own_b, own_c = ga.own, gb.own, gc.own
+    other_a, other_b, other_c = ga.other, gb.other, gc.other
     ids_array = jnp.array(ids, jnp.int32)
     owners = jnp.bitwise_xor(ids_array, me)
     places = jnp.stack([owners * 2 + core, owners * 2 + 1 - core]).astype(jnp.int32)
@@ -493,23 +564,24 @@
         parts = matrix.astype(bf16).reshape(2, count, size, width)
         return parts[0], parts[1]
 
-    def reduce_chunk(own, other):
-        return scatter_chunk(own + swap_core(other))
-
     g_value_own, g_value_other = split(outer_sum(squared, grad_carried), hu)
-    sum_c = reduce_chunk(g_value_own, g_value_other)
+    rc = Scatter(g_value_own, g_value_other)
 
     carried = dot(squared, hidden_value_w)
     block_out = (hidden + gate * carried).astype(bf16)
     grad_gate_pre = (grad_out * carried * gate * (1.0 - gate)).astype(bf16)
     grad_pre = (against(grad_carried, hidden_value_w) * 2.0 * ffn_relu).astype(bf16)
+    rc.corner()
+    grad_pre = after(grad_pre, rc.far)
     g_key_own, g_key_other = split(outer_sum(grad_pre, ffn_key_in), hu)
     g_recept_own, g_recept_other = unplace(
         [outer_sum(grad_gate_pre, ffn_recept_in).astype(bf16)], places, ((0, hc),), count
     )
-    sum_b = reduce_chunk(
+    rb = Scatter(
         jnp.concatenate([g_key_own, g_recept_own], 1), jnp.concatenate([g_key_other, g_recept_other], 1)
     )
+    grad_gate_pre = after(grad_gate_pre, *rc.seen)
+    rc.edge()
     grad_key_two = dot(grad_pre, hidden_key_t)
     grad_recept_two = dot(grad_gate_pre, hidden_recept_t)
 
@@ -524,6 +596,9 @@
     grad_second, ffn_small = blend_back(
         low, prior, (grad_key_two, grad_recept_two), (channel_key, channel_recept)
     )
+    grad_second = after(grad_second, *rc.seen, rb.far)
+    rb.corner()
+    rc.near()
     grad_second_gain = jnp.sum(grad_second * scaled_two, axis=0)
     grad_second_bias = jnp.sum(grad_second, axis=0)
     grad_hidden = grad_out + norm_back(grad_second, scaled_two, inverse_two, second_gain)
@@ -533,6 +608,9 @@
     grad_gated = against(grad_attended, output_w)
     grad_mixed = grad_gated * opened
     grad_recept = (grad_gated * mixed * opened * (1.0 - opened)).astype(bf16)
+    grad_mixed = after(grad_mixed, *rb.seen, *rc.seen)
+    rc.wide()
+    rb.edge()
     back_end = call_whole(
         backward_end_kernel, pair, grad_mixed, keys, mixed, state_b, cols_up, rates
     )
@@ -556,10 +634,12 @@
     )
     grad_keys = grad_keys_full.astype(bf16)
     grad_values = grad_values_full.astype(bf16)
+    grad_keys = after(grad_keys, *rb.seen, *rc.seen)
+    rb.near()
     g_key = outer_sum(grad_keys, mix_key).astype(bf16)
     g_value = outer_sum(grad_values, mix_value).astype(bf16)
     g_recept = outer_sum(grad_recept, mix_recept).astype(bf16)
-    sum_a = reduce_chunk(
+    ra = Scatter(
         *unplace(
             [g_key, g_value, g_recept, g_output],
             places,
@@ -567,6 +647,8 @@
             count,
         )
     )
+    grad_keys = after(grad_keys, *rb.seen)
+    rb.wide()
     grad_key_one = dot(grad_keys, key_t)
     grad_value_one = dot(grad_values, value_t)
     grad_recept_one = dot(grad_recept, recept_t)
@@ -576,6 +658,10 @@
         (grad_key_one, grad_value_one, grad_recept_one),
         (blend_key, blend_value, blend_recept),
     )
+    ra.corner()
+    ra.edge()
+    ra.near()
+    ra.wide()
     grad_first_gain = jnp.sum(grad_normed * scaled_one, axis=0)
     grad_first_bias = jnp.sum(grad_normed, axis=0)
     grad_tokens = grad_hidden + norm_back(grad_normed, scaled_one, inverse_one, first_gain)
@@ -613,7 +699,7 @@
 
         return take
 
-    take_a, take_b, take_c = finish(sum_a), finish(sum_b), finish(sum_c)
+    take_a, take_b, take_c = finish(ra.sum), finish(rb.sum), finish(rc.sum)
     return (
         block_out,
         grad_tokens,

time: 1150 us -> 515 us (0.45)
  Pallas kernels: 660 us -> 40.2 us
  starting transfers between devices: 133 us -> 98.9 us
  matrix products: 64 us -> 43.6 us
  local copies, waits for them, and re-layouts: 74.8 us -> 90.7 us
  other arithmetic: 58.9 us -> 72.6 us
    pallas_call x2, Pallas kernels: 323 us -> 12.1 us  [place(): pl.pallas_call(functools.partial(place_kernel, pieces, count), out_shape=...]
    pallas_call x2, Pallas kernels: 323 us -> 13.4 us  [unplace(): pl.pallas_call(functools.partial(unplace_kernel, pieces, count), out_shap...]
    ppermute x66, starting transfers between devices: 76.4 us -> 51.9 us  [swap(): return lax.ppermute(value, 'mp', [(i, i ^ 1 << bit) for i in range(count)])]
    unnamed x163 -> x213, local copies, waits for them, and re-layouts: 38.8 us -> 53.2 us
    add x15 -> x14, other arithmetic: 25.1 us -> 34.5 us  [the longest x3 17.6 us: corner(): part = self.own + self.far]
  transfers between devices with their start and end apart: 84 -> 84, of which waited for: 38 -> 42; matrix products, arithmetic and copies ran while one was open for 13% -> 33% of each run, Pallas kernels for 58% -> 6%
where the time goes in v2:
time: 515 us; the launch traced here: 511 us
  waiting for transfers between devices  161 us (31%)
  starting transfers between devices  98.9 us (19%)
  local copies, waits for them, and re-layouts  90.7 us (18%)
  other arithmetic  72.6 us (14%)
  matrix products  43.6 us (8%)
  Pallas kernels  40.2 us (8%)
    ppermute x66, waiting for transfers between devices, swap(): return lax.ppermute(value, 'mp', [(i, i ^ 1 << bit) for i in range(count)])  146 us
    unnamed x213, local copies, waits for them, and re-layouts  53.2 us
    ppermute x66, starting transfers between devices, swap(): return lax.ppermute(value, 'mp', [(i, i ^ 1 << bit) for i in range(count)])  51.9 us
    ppermute x9, starting transfers between devices, swap_core(): return lax.ppermute(value, 'dp', [(i, i ^ 1) for i in range(count)])  29.5 us
    dot_general x7, matrix products, dot(): return jnp.dot(left, right, preferred_element_type=f32)  19.5 us
    add x3, other arithmetic, corner(): part = self.own + self.far  17.6 us
    ppermute x5, waiting for transfers between devices, total_small(): lax.ppermute(value, axis, [(i, i ^ 1 << bit) for i in range(count)])  15 us
    pallas_call x4, Pallas kernels, call_whole(): pl.pallas_call(kernel, out_shape=outs, in_specs=[pl.BlockSpec(memory_spac...  14.7 us
  transfers between devices with their start and end apart: 84, of which 42 were waited for; matrix products, arithmetic and copies ran while one was open for 33% of the time, Pallas kernels for 6%

profile of v2, /device:TPU:1, one launch (start us, length us, event | category | flops | bytes accessed | tf_op | source)
XLA Modules:
  0.0 510.9 jit_solution(608844469455130226)
XLA Ops:
  3.0 3.2 collective-permute-start.20
  18.6 13.2 %collective-permute-done.1 = bf16[1,128,1024]{2,1,0:T(8,128)(2,1)S(1)} collective-permute-done((bf16[1,128,1024]{2,1,0:T(8,128)(2,1)S(1)}, bf16[1,128,1024]{2,1,0:T(8,128)(2,1)S(1)}, u32[]{:S(2)}, u32[]{:S(2)}) %collective-permute-start.1) | collective-permute-done | bytes 262176 | tf_op jit(solution)/shard_map/ppermute | solution.py:24
  37.2 2.7 collective-permute-start
  39.9 5.7 %collective-permute-done.3 = bf16[2,128,1024]{2,1,0:T(8,128)(2,1)S(1)} collective-permute-done((bf16[2,128,1024]{2,1,0:T(8,128)(2,1)}, bf16[2,128,1024]{2,1,0:T(8,128)(2,1)S(1)}, u32[]{:S(2)}, u32[]{:S(2)}) %collective-permute-start.3) | collective-permute-done | bytes 524320 | tf_op jit(solution)/shard_map/ppermute | solution.py:24
  47.1 2.5 collective-permute-start.7
  54.9 2.7 collective-permute-done.6
  67.2 4.2 collective-permute-start.10
  77.9 12.3 %collective-permute-done.13 = f32[4,2,64]{2,1,0:T(2,128)S(1)} collective-permute-done((f32[4,2,64]{2,1,0:T(2,128)S(1)}, f32[4,2,64]{2,1,0:T(2,128)S(1)}, u32[]{:S(2)}, u32[]{:S(2)}) %collective-permute-start.13) | collective-permute-done | bytes 2080 | tf_op jit(solution)/shard_map/ppermute | solution.py:24
  90.3 3.1 collective-permute-start.30
  102.1 6.2 %collective-permute-done.25 = bf16[2,160,1024]{2,1,0:T(8,128)(2,1)S(1)} collective-permute-done((bf16[2,160,1024]{2,1,0:T(8,128)(2,1)}, bf16[2,160,1024]{2,1,0:T(8,128)(2,1)S(1)}, u32[]{:S(2)}, u32[]{:S(2)}) %collective-permute-start.25) | collective-permute-done | bytes 655392 | tf_op jit(solution)/shard_map/ppermute | solution.py:24
  108.6 6.4 %collective-permute-done.26 = bf16[2,160,1024]{2,1,0:T(8,128)(2,1)S(1)} collective-permute-done((bf16[2,160,1024]{2,1,0:T(8,128)(2,1)}, bf16[2,160,1024]{2,1,0:T(8,128)(2,1)S(1)}, u32[]{:S(2)}, u32[]{:S(2)}) %collective-permute-start.26) | collective-permute-done | bytes 655392 | tf_op jit(solution)/shard_map/ppermute | solution.py:24
  118.3 3.4 collective-permute-done.27
  123.2 3.4 collective-permute-start.29
  129.5 12.9 %collective-permute-done.32 = bf16[2,128,1024]{2,1,0:T(8,128)(2,1)S(1)} collective-permute-done((bf16[2,128,1024]{2,1,0:T(8,128)(2,1)}, bf16[2,128,1024]{2,1,0:T(8,128)(2,1)S(1)}, u32[]{:S(2)}, u32[]{:S(2)}) %collective-permute-start.32) | collective-permute-done | bytes 524320 | tf_op jit(solution)/shard_map/ppermute | solution.py:24
  150.3 2.5 slice.454
  152.8 2.6 collective-permute-done.35
  162.8 3.3 collective-permute-start.39
  166.2 8.6 %shard_map.365 = (bf16[1024,1024]{1,0:T(8,128)(2,1)S(1)}, bf16[1024,1024]{1,0:T(8,128)(2,1)S(1)}, bf16[1024,1024]{1,0:T(8,128)(2,1)S(1)}, bf16[1024,1024]{1,0:T(8,128)(2,1)S(1)}) custom-call(s32[2,16]{1,0:T(2,128)S(1)} %pad_add_fusion.places_ref, bf16[16,128,1024]{2,1,0:T(8,128)(2,1)S(1)} %copy-done.6, bf16[16,128,1024]{2,1,0:T(8,128)(2,1)} %collective-permute-done.10.other_ref), custom_call_target="tpu_custom_call" | custom-call | bytes 48000000 | tf_op jit(solution)/shard_map/pallas_call | solution.py:165
  175.7 2.9 fusion.87.v_ref
  178.6 3.3 shard_map.366
  184.9 2.3 collective-permute-done.16
  187.2 2.7 collective-permute-done.17
  190.2 4.4 collective-permute-done.18
  194.6 4.0 shard_map.367
  204.5 2.7 collective-permute-start.19
  207.2 4.7 slice.455
  211.9 7.5 %pad_maximum_fusion = bf16[32,128,1024]{2,1,0:T(8,128)(2,1)} fusion(bf16[16,128,1024]{2,1,0:T(8,128)(2,1)} %slice.455, bf16[16,128,1024]{2,1,0:T(8,128)(2,1)} %slice.454), kind=kLoop, calls=%fused_computation.1 | loop fusion | flops 4194304 | bytes 16777216 | tf_op jit(solution)/shard_map/concatenate | solution.py:555
  219.5 2.5 copy-done.3
  222.0 3.5 shard_map.368
  226.8 2.9 copy-done.52
  229.6 2.5 convolution_maximum_fusion
  232.2 2.4 convolution_convert_fusion.1
  234.6 3.9 fusion.98
  238.4 4.6 collective-permute-start.40
  243.1 4.9 constant_dynamic-update-slice_fusion.40
  248.0 7.0 %fusion.26 = (bf16[256,1024]{1,0:T(8,128)(2,1)S(1)}, bf16[256,1024]{1,0:T(8,128)(2,1)}) fusion(f32[256,1024]{1,0:T(8,128)S(1)} %fusion.4, bf16[256,1024]{1,0:T(8,128)(2,1)S(1)} %copy-done.53, f32[256,1024]{1,0:T(8,128)S(1)} %copy-done.32, bf16[4096,1024]{1,0:T(8,128)(2,1)} %bitcast.233, f32[256,4096]{1,0:T(8,128)S(1)} %convolution_maximum_fusion), kind=kOutput, calls=%fused_computation.54 | convolution fusion | flops 2151940096 | bytes 16252928 | tf_op jit(solution)/shard_map/dot_general | solution.py:367
  256.8 4.2 shard_map.369
  262.0 3.8 fusion.1
  265.7 4.2 convolution_convert_fusion
  270.0 3.7 fusion.97
  273.7 5.4 %pad_maximum_fusion.1 = bf16[16,160,1024]{2,1,0:T(8,128)(2,1)} fusion(bf16[16,32,1024]{2,1,0:T(8,128)(2,1)S(1)} %get-tuple-element.52, bf16[16,128,1024]{2,1,0:T(8,128)(2,1)} %bitcast.219), kind=kLoop, calls=%fused_computation.7 | loop fusion | flops 10485760 | bytes 10485760 | tf_op jit(solution)/shard_map/concatenate | solution.py:581
  279.2 4.3 add.369
  290.9 3.2 collective-permute-done.41
  298.3 5.9 %fusion.103 = f32[256,1024]{1,0:T(8,128)S(1)} fusion(bf16[256,4096]{1,0:T(8,128)(2,1)S(1)} %copy-done.45, bf16[4096,1024]{1,0:T(8,128)(2,1)} %bitcast.237), kind=kOutput, calls=%fused_computation.339 | convolution fusion | flops 2147483648 | bytes 11534336 | tf_op jit(solution)/shard_map/dot_general | solution.py:367
  309.3 2.7 slice_add_fusion.9
  318.9 3.4 collective-permute-done.50
  329.3 8.9 %maximum_add_fusion = bf16[16,160,1024]{2,1,0:T(8,128)(2,1)} fusion(bf16[16,160,1024]{2,1,0:T(8,128)(2,1)} %collective-permute-done.47, bf16[16,32,1024]{2,1,0:T(8,128)(2,1)S(1)} %copy-done.30, bf16[16,128,1024]{2,1,0:T(8,128)(2,1)} %bitcast.220), kind=kLoop, calls=%fused_computation.8 | loop fusion | flops 15728640 | bytes 15728640 | tf_op jit(solution)/shard_map/add | solution.py:86
  348.8 3.5 shard_map.370
  355.8 4.4 collective-permute-done.53
  361.3 3.4 collective-permute-done.54
  365.1 2.9 collective-permute-done.55
  368.3 4.4 collective-permute-done.56
  372.8 4.0 shard_map.371
  380.9 9.2 %shard_map.372 = (bf16[16,128,1024]{2,1,0:T(8,128)(2,1)S(1)}, bf16[16,128,1024]{2,1,0:T(8,128)(2,1)}) custom-call(s32[2,16]{1,0:T(2,128)S(1)} %pad_add_fusion.places_ref, bf16[1024,1024]{1,0:T(8,128)(2,1)S(1)} %convolution_convert_fusion.5.rest_0_, bf16[1024,1024]{1,0:T(8,128)(2,1)S(1)} %convolution_convert_fusion.4.rest_1_, ...), custom_call_target="tpu_custom_call" | custom-call | bytes 48000000 | tf_op jit(solution)/shard_map/pallas_call | solution.py:202
  392.1 9.9 %collective-permute-start.70 = (bf16[16,128,1024]{2,1,0:T(8,128)(2,1)}, bf16[16,128,1024]{2,1,0:T(8,128)(2,1)}, u32[]{:S(2)}, u32[]{:S(2)}) collective-permute-start(bf16[16,128,1024]{2,1,0:T(8,128)(2,1)} %get-tuple-element.65), channel_id=1, source_target_pairs={{0,16},{16,0},{1,17},{17,1},{2,18},{18,2},{3,19},{19,3},{4,20},{20... | collective-permute-start | bytes 12582920 | tf_op jit(solution)/shard_map/ppermute | solution.py:29
  402.0 2.4 slice_add_fusion.1
  411.0 9.8 %collective-permute-done.61 = bf16[2,160,1024]{2,1,0:T(8,128)(2,1)S(1)} collective-permute-done((bf16[2,160,1024]{2,1,0:T(8,128)(2,1)S(1)}, bf16[2,160,1024]{2,1,0:T(8,128)(2,1)S(1)}, u32[]{:S(2)}, u32[]{:S(2)}) %collective-permute-start.61) | collective-permute-done | bytes 655392 | tf_op jit(solution)/shard_map/ppermute | solution.py:24
  423.3 4.4 add.406
  443.6 4.2 collective-permute-done.72
  454.3 4.0 collective-permute-done.67
  458.3 3.8 collective-permute-start.68
  462.1 10.0 %collective-permute-done.68 = f32[11,1024]{1,0:T(8,128)S(1)} collective-permute-done((f32[11,1024]{1,0:T(8,128)S(1)}, f32[11,1024]{1,0:T(8,128)S(1)}, u32[]{:S(2)}, u32[]{:S(2)}) %collective-permute-start.68) | collective-permute-done | bytes 45088 | tf_op jit(solution)/shard_map/ppermute | solution.py:129
  478.1 9.3 %collective-permute-done.78 = bf16[2,128,1024]{2,1,0:T(8,128)(2,1)S(1)} collective-permute-done((bf16[2,128,1024]{2,1,0:T(8,128)(2,1)S(1)}, bf16[2,128,1024]{2,1,0:T(8,128)(2,1)S(1)}, u32[]{:S(2)}, u32[]{:S(2)}) %collective-permute-start.78) | collective-permute-done | bytes 524320 | tf_op jit(solution)/shard_map/ppermute | solution.py:24
  493.5 10.2 %collective-permute-done.79 = bf16[1,128,1024]{2,1,0:T(8,128)(2,1)S(1)} collective-permute-done((bf16[1,128,1024]{2,1,0:T(8,128)(2,1)S(1)}, bf16[1,128,1024]{2,1,0:T(8,128)(2,1)S(1)}, u32[]{:S(2)}, u32[]{:S(2)}) %collective-permute-start.79) | collective-permute-done | bytes 262176 | tf_op jit(solution)/shard_map/ppermute | solution.py:24
  (550 shorter events, 189.5 us)
Async XLA Ops:
  3.0 68.4 %collective-permute-start.20 = (bf16[1,160,1024]{2,1,0:T(8,128)(2,1)S(1)}, bf16[1,160,1024]{2,1,0:T(8,128)(2,1)S(1)}, u32[]{:S(2)}, u32[]{:S(2)}) collective-permute-start(bf16[1,160,1024]{2,1,0:T(8,128)(2,1)S(1)} %maximum_bitcast_fusion), channel_id=1, source_target_pairs={{0,8},{1,9},{2,10},{3,11},{4,12},{5,13},{6,14},{7,15},{8,0},{9,1},... | collective-permute-start | bytes 983048 | tf_op jit(solution)/shard_map/ppermute | solution.py:24
  8.8 23.1 %collective-permute-start.1 = (bf16[1,128,1024]{2,1,0:T(8,128)(2,1)S(1)}, bf16[1,128,1024]{2,1,0:T(8,128)(2,1)S(1)}, u32[]{:S(2)}, u32[]{:S(2)}) collective-permute-start(bf16[1,128,1024]{2,1,0:T(8,128)(2,1)S(1)} %maximum_bitcast_fusion.1), channel_id=1, source_target_pairs={{0,8},{1,9},{2,10},{3,11},{4,12},{5,13},{6,14},{7,15},{8,0},{9,1},... | collective-permute-start | bytes 786440 | tf_op jit(solution)/shard_map/ppermute | solution.py:24
  9.5 27.7 %collective-permute-start.11 = (f32[1,2,64]{2,1,0:T(2,128)S(1)}, f32[1,2,64]{2,1,0:T(2,128)S(1)}, u32[]{:S(2)}, u32[]{:S(2)}) collective-permute-start(f32[1,2,64]{2,1,0:T(2,128)S(1)} %maximum_bitcast_fusion.2), channel_id=1, source_target_pairs={{0,1},{1,0},{2,3},{3,2},{4,5},{5,4},{6,7},{7,6},{8,9},{9,8},{10,11... | collective-permute-start | bytes 1544 | tf_op jit(solution)/shard_map/ppermute | solution.py:24
  32.7 14.4 %collective-permute-start.2 = (bf16[2,128,1024]{2,1,0:T(8,128)(2,1)}, bf16[2,128,1024]{2,1,0:T(8,128)(2,1)}, u32[]{:S(2)}, u32[]{:S(2)}) collective-permute-start(bf16[2,128,1024]{2,1,0:T(8,128)(2,1)} %pad_maximum_fusion.6), channel_id=1, source_target_pairs={{0,1},{1,0},{2,3},{3,2},{4,5},{5,4},{6,7},{7,6},{8,9},{9,8},{10,11... | collective-permute-start | bytes 1572872 | tf_op jit(solution)/shard_map/ppermute | solution.py:24
  33.7 11.9 %collective-permute-start.3 = (bf16[2,128,1024]{2,1,0:T(8,128)(2,1)}, bf16[2,128,1024]{2,1,0:T(8,128)(2,1)S(1)}, u32[]{:S(2)}, u32[]{:S(2)}) collective-permute-start(bf16[2,128,1024]{2,1,0:T(8,128)(2,1)} %pad_maximum_fusion.6), channel_id=1, source_target_pairs={{0,2},{1,3},{2,0},{3,1},{4,6},{5,7},{6,4},{7,5},{8,10},{9,11},{10,... | collective-permute-start | bytes 1572872 | tf_op jit(solution)/shard_map/ppermute | solution.py:24
  34.9 11.9 %collective-permute-start.4 = (bf16[2,128,1024]{2,1,0:T(8,128)(2,1)}, bf16[2,128,1024]{2,1,0:T(8,128)(2,1)}, u32[]{:S(2)}, u32[]{:S(2)}) collective-permute-start(bf16[2,128,1024]{2,1,0:T(8,128)(2,1)} %pad_maximum_fusion.6), channel_id=1, source_target_pairs={{0,4},{1,5},{2,6},{3,7},{4,0},{5,1},{6,2},{7,3},{8,12},{9,13},{10,... | collective-permute-start | bytes 1572872 | tf_op jit(solution)/shard_map/ppermute | solution.py:24
  37.2 38.1 %collective-permute-start = (bf16[1,1024]{1,0:T(2,128)(2,1)S(1)}, bf16[1,1024]{1,0:T(2,128)(2,1)S(1)}, u32[]{:S(2)}, u32[]{:S(2)}) collective-permute-start(bf16[1,1024]{1,0:T(2,128)(2,1)S(1)} %slice.337), channel_id=1, source_target_pairs={{0,1},{1,2},{2,3},{3,4},{4,5},{5,6},{6,7},{7,8},{8,9},{9,10},{10,1... | collective-permute-start | bytes 6152 | tf_op jit(solution)/shard_map/ppermute | solution.py:509
  45.6 15.2 %collective-permute-start.5 = (bf16[2,128,1024]{2,1,0:T(8,128)(2,1)S(1)}, bf16[2,128,1024]{2,1,0:T(8,128)(2,1)S(1)}, u32[]{:S(2)}, u32[]{:S(2)}) collective-permute-start(bf16[2,128,1024]{2,1,0:T(8,128)(2,1)S(1)} %collective-permute-done.3), channel_id=1, source_target_pairs={{0,1},{1,0},{2,3},{3,2},{4,5},{5,4},{6,7},{7,6},{8,9},{9,8},{10,11... | collective-permute-start | bytes 1572872 | tf_op jit(solution)/shard_map/ppermute | solution.py:24
  46.8 10.8 %collective-permute-start.6 = (bf16[2,128,1024]{2,1,0:T(8,128)(2,1)}, bf16[2,128,1024]{2,1,0:T(8,128)(2,1)S(1)}, u32[]{:S(2)}, u32[]{:S(2)}) collective-permute-start(bf16[2,128,1024]{2,1,0:T(8,128)(2,1)} %collective-permute-done.4), channel_id=1, source_target_pairs={{0,2},{1,3},{2,0},{3,1},{4,6},{5,7},{6,4},{7,5},{8,10},{9,11},{10,... | collective-permute-start | bytes 1572872 | tf_op jit(solution)/shard_map/ppermute | solution.py:24
  47.1 12.5 %collective-permute-start.7 = (bf16[2,128,1024]{2,1,0:T(8,128)(2,1)}, bf16[2,128,1024]{2,1,0:T(8,128)(2,1)S(1)}, u32[]{:S(2)}, u32[]{:S(2)}) collective-permute-start(bf16[2,128,1024]{2,1,0:T(8,128)(2,1)} %collective-permute-done.2), channel_id=1, source_target_pairs={{0,4},{1,5},{2,6},{3,7},{4,0},{5,1},{6,2},{7,3},{8,12},{9,13},{10,... | collective-permute-start | bytes 1572872 | tf_op jit(solution)/shard_map/ppermute | solution.py:24
  57.7 15.8 %collective-permute-start.12 = (f32[2,2,64]{2,1,0:T(2,128)S(1)}, f32[2,2,64]{2,1,0:T(2,128)S(1)}, u32[]{:S(2)}, u32[]{:S(2)}) collective-permute-start(f32[2,2,64]{2,1,0:T(2,128)S(1)} %pad_maximum_fusion.24), channel_id=1, source_target_pairs={{0,2},{1,3},{2,0},{3,1},{4,6},{5,7},{6,4},{7,5},{8,10},{9,11},{10,... | collective-permute-start | bytes 3080 | tf_op jit(solution)/shard_map/ppermute | solution.py:24
  67.2 99.0 %collective-permute-start.10 = (bf16[16,128,1024]{2,1,0:T(8,128)(2,1)}, bf16[16,128,1024]{2,1,0:T(8,128)(2,1)}, u32[]{:S(2)}, u32[]{:S(2)}) collective-permute-start(bf16[16,128,1024]{2,1,0:T(8,128)(2,1)} %constant_dynamic-update-slice_fusion.own_ref), channel_id=1, source_target_pairs={{0,16},{16,0},{1,17},{17,1},{2,18},{18,2},{3,19},{19,3},{4,20},{20... | collective-permute-start | bytes 12582920 | tf_op jit(solution)/shard_map/ppermute | solution.py:29
  72.3 22.9 %collective-permute-start.21 = (bf16[2,160,1024]{2,1,0:T(8,128)(2,1)}, bf16[2,160,1024]{2,1,0:T(8,128)(2,1)}, u32[]{:S(2)}, u32[]{:S(2)}) collective-permute-start(bf16[2,160,1024]{2,1,0:T(8,128)(2,1)} %pad_maximum_fusion.2), channel_id=1, source_target_pairs={{0,1},{1,0},{2,3},{3,2},{4,5},{5,4},{6,7},{7,6},{8,9},{9,8},{10,11... | collective-permute-start | bytes 1966088 | tf_op jit(solution)/shard_map/ppermute | solution.py:24
  72.7 20.7 %collective-permute-start.22 = (bf16[2,160,1024]{2,1,0:T(8,128)(2,1)}, bf16[2,160,1024]{2,1,0:T(8,128)(2,1)S(1)}, u32[]{:S(2)}, u32[]{:S(2)}) collective-permute-start(bf16[2,160,1024]{2,1,0:T(8,128)(2,1)} %pad_maximum_fusion.2), channel_id=1, source_target_pairs={{0,2},{1,3},{2,0},{3,1},{4,6},{5,7},{6,4},{7,5},{8,10},{9,11},{10,... | collective-permute-start | bytes 1966088 | tf_op jit(solution)/shard_map/ppermute | solution.py:24
  73.4 20.3 %collective-permute-start.23 = (bf16[2,160,1024]{2,1,0:T(8,128)(2,1)}, bf16[2,160,1024]{2,1,0:T(8,128)(2,1)}, u32[]{:S(2)}, u32[]{:S(2)}) collective-permute-start(bf16[2,160,1024]{2,1,0:T(8,128)(2,1)} %pad_maximum_fusion.2), channel_id=1, source_target_pairs={{0,4},{1,5},{2,6},{3,7},{4,0},{5,1},{6,2},{7,3},{8,12},{9,13},{10,... | collective-permute-start | bytes 1966088 | tf_op jit(solution)/shard_map/ppermute | solution.py:24
  75.3 15.0 %collective-permute-start.13 = (f32[4,2,64]{2,1,0:T(2,128)S(1)}, f32[4,2,64]{2,1,0:T(2,128)S(1)}, u32[]{:S(2)}, u32[]{:S(2)}) collective-permute-start(f32[4,2,64]{2,1,0:T(2,128)S(1)} %pad_maximum_fusion.23), channel_id=1, source_target_pairs={{0,4},{1,5},{2,6},{3,7},{4,0},{5,1},{6,2},{7,3},{8,12},{9,13},{10,... | collective-permute-start | bytes 6152 | tf_op jit(solution)/shard_map/ppermute | solution.py:24
  90.3 36.9 %collective-permute-start.30 = (bf16[1,128,1024]{2,1,0:T(8,128)(2,1)S(1)}, bf16[1,128,1024]{2,1,0:T(8,128)(2,1)S(1)}, u32[]{:S(2)}, u32[]{:S(2)}) collective-permute-start(bf16[1,128,1024]{2,1,0:T(8,128)(2,1)S(1)} %get-tuple-element.186), channel_id=1, source_target_pairs={{0,8},{1,9},{2,10},{3,11},{4,12},{5,13},{6,14},{7,15},{8,0},{9,1},... | collective-permute-start | bytes 786440 | tf_op jit(solution)/shard_map/ppermute | solution.py:24
  93.4 21.6 %collective-permute-start.24 = (bf16[2,160,1024]{2,1,0:T(8,128)(2,1)S(1)}, bf16[2,160,1024]{2,1,0:T(8,128)(2,1)S(1)}, u32[]{:S(2)}, u32[]{:S(2)}) collective-permute-start(bf16[2,160,1024]{2,1,0:T(8,128)(2,1)S(1)} %collective-permute-done.22), channel_id=1, source_target_pairs={{0,1},{1,0},{2,3},{3,2},{4,5},{5,4},{6,7},{7,6},{8,9},{9,8},{10,11... | collective-permute-start | bytes 1966088 | tf_op jit(solution)/shard_map/ppermute | solution.py:24
  93.7 14.5 %collective-permute-start.25 = (bf16[2,160,1024]{2,1,0:T(8,128)(2,1)}, bf16[2,160,1024]{2,1,0:T(8,128)(2,1)S(1)}, u32[]{:S(2)}, u32[]{:S(2)}) collective-permute-start(bf16[2,160,1024]{2,1,0:T(8,128)(2,1)} %collective-permute-done.23), channel_id=1, source_target_pairs={{0,2},{1,3},{2,0},{3,1},{4,6},{5,7},{6,4},{7,5},{8,10},{9,11},{10,... | collective-permute-start | bytes 1966088 | tf_op jit(solution)/shard_map/ppermute | solution.py:24
  95.2 19.8 %collective-permute-start.26 = (bf16[2,160,1024]{2,1,0:T(8,128)(2,1)}, bf16[2,160,1024]{2,1,0:T(8,128)(2,1)S(1)}, u32[]{:S(2)}, u32[]{:S(2)}) collective-permute-start(bf16[2,160,1024]{2,1,0:T(8,128)(2,1)} %collective-permute-done.21), channel_id=1, source_target_pairs={{0,4},{1,5},{2,6},{3,7},{4,0},{5,1},{6,2},{7,3},{8,12},{9,13},{10,... | collective-permute-start | bytes 1966088 | tf_op jit(solution)/shard_map/ppermute | solution.py:24
  108.3 18.4 %collective-permute-start.14 = (f32[8,2,64]{2,1,0:T(2,128)S(1)}, f32[8,2,64]{2,1,0:T(2,128)S(1)}, u32[]{:S(2)}, u32[]{:S(2)}) collective-permute-start(f32[8,2,64]{2,1,0:T(2,128)S(1)} %pad_maximum_fusion.22), channel_id=1, source_target_pairs={{0,8},{1,9},{2,10},{3,11},{4,12},{5,13},{6,14},{7,15},{8,0},{9,1},... | collective-permute-start | bytes 12296 | tf_op jit(solution)/shard_map/ppermute | solution.py:24
  115.0 7.4 %collective-permute-start.28 = (bf16[1,160,1024]{2,1,0:T(8,128)(2,1)S(1)}, bf16[1,160,1024]{2,1,0:T(8,128)(2,1)S(1)}, u32[]{:S(2)}, u32[]{:S(2)}) collective-permute-start(bf16[1,160,1024]{2,1,0:T(8,128)(2,1)S(1)} %slice.453), channel_id=1, source_target_pairs={{0,2},{1,3},{2,0},{3,1},{4,6},{5,7},{6,4},{7,5},{8,10},{9,11},{10,... | collective-permute-start | bytes 983048 | tf_op jit(solution)/shard_map/ppermute | solution.py:24
  123.2 84.0 %collective-permute-start.29 = (bf16[16,160,1024]{2,1,0:T(8,128)(2,1)}, bf16[16,160,1024]{2,1,0:T(8,128)(2,1)}, u32[]{:S(2)}, u32[]{:S(2)}) collective-permute-start(bf16[16,160,1024]{2,1,0:T(8,128)(2,1)} %constant_dynamic-update-slice_fusion.20.own_ref), channel_id=1, source_target_pairs={{0,16},{16,0},{1,17},{17,1},{2,18},{18,2},{3,19},{19,3},{4,20},{20... | collective-permute-start | bytes 15728648 | tf_op jit(solution)/shard_map/ppermute | solution.py:29
  128.1 15.5 %collective-permute-start.31 = (bf16[2,128,1024]{2,1,0:T(8,128)(2,1)}, bf16[2,128,1024]{2,1,0:T(8,128)(2,1)}, u32[]{:S(2)}, u32[]{:S(2)}) collective-permute-start(bf16[2,128,1024]{2,1,0:T(8,128)(2,1)} %pad_maximum_fusion.8), channel_id=1, source_target_pairs={{0,1},{1,0},{2,3},{3,2},{4,5},{5,4},{6,7},{7,6},{8,9},{9,8},{10,11... | collective-permute-start | bytes 1572872 | tf_op jit(solution)/shard_map/ppermute | solution.py:24
  128.9 13.6 %collective-permute-start.32 = (bf16[2,128,1024]{2,1,0:T(8,128)(2,1)}, bf16[2,128,1024]{2,1,0:T(8,128)(2,1)S(1)}, u32[]{:S(2)}, u32[]{:S(2)}) collective-permute-start(bf16[2,128,1024]{2,1,0:T(8,128)(2,1)} %pad_maximum_fusion.8), channel_id=1, source_target_pairs={{0,2},{1,3},{2,0},{3,1},{4,6},{5,7},{6,4},{7,5},{8,10},{9,11},{10,... | collective-permute-start | bytes 1572872 | tf_op jit(solution)/shard_map/ppermute | solution.py:24
  128.9 14.2 %collective-permute-start.33 = (bf16[2,128,1024]{2,1,0:T(8,128)(2,1)}, bf16[2,128,1024]{2,1,0:T(8,128)(2,1)}, u32[]{:S(2)}, u32[]{:S(2)}) collective-permute-start(bf16[2,128,1024]{2,1,0:T(8,128)(2,1)} %pad_maximum_fusion.8), channel_id=1, source_target_pairs={{0,4},{1,5},{2,6},{3,7},{4,0},{5,1},{6,2},{7,3},{8,12},{9,13},{10,... | collective-permute-start | bytes 1572872 | tf_op jit(solution)/shard_map/ppermute | solution.py:24
  142.4 14.3 %collective-permute-start.34 = (bf16[2,128,1024]{2,1,0:T(8,128)(2,1)S(1)}, bf16[2,128,1024]{2,1,0:T(8,128)(2,1)S(1)}, u32[]{:S(2)}, u32[]{:S(2)}) collective-permute-start(bf16[2,128,1024]{2,1,0:T(8,128)(2,1)S(1)} %collective-permute-done.32), channel_id=1, source_target_pairs={{0,1},{1,0},{2,3},{3,2},{4,5},{5,4},{6,7},{7,6},{8,9},{9,8},{10,11... | collective-permute-start | bytes 1572872 | tf_op jit(solution)/shard_map/ppermute | solution.py:24
  143.1 12.3 %collective-permute-start.35 = (bf16[2,128,1024]{2,1,0:T(8,128)(2,1)}, bf16[2,128,1024]{2,1,0:T(8,128)(2,1)S(1)}, u32[]{:S(2)}, u32[]{:S(2)}) collective-permute-start(bf16[2,128,1024]{2,1,0:T(8,128)(2,1)} %collective-permute-done.33), channel_id=1, source_target_pairs={{0,2},{1,3},{2,0},{3,1},{4,6},{5,7},{6,4},{7,5},{8,10},{9,11},{10,... | collective-permute-start | bytes 1572872 | tf_op jit(solution)/shard_map/ppermute | solution.py:24
  143.6 12.8 %collective-permute-start.36 = (bf16[2,128,1024]{2,1,0:T(8,128)(2,1)}, bf16[2,128,1024]{2,1,0:T(8,128)(2,1)S(1)}, u32[]{:S(2)}, u32[]{:S(2)}) collective-permute-start(bf16[2,128,1024]{2,1,0:T(8,128)(2,1)} %collective-permute-done.31), channel_id=1, source_target_pairs={{0,4},{1,5},{2,6},{3,7},{4,0},{5,1},{6,2},{7,3},{8,12},{9,13},{10,... | collective-permute-start | bytes 1572872 | tf_op jit(solution)/shard_map/ppermute | solution.py:24
  162.8 80.2 %collective-permute-start.39 = (bf16[16,128,1024]{2,1,0:T(8,128)(2,1)}, bf16[16,128,1024]{2,1,0:T(8,128)(2,1)}, u32[]{:S(2)}, u32[]{:S(2)}) collective-permute-start(bf16[16,128,1024]{2,1,0:T(8,128)(2,1)} %get-tuple-element.251), channel_id=1, source_target_pairs={{0,16},{16,0},{1,17},{17,1},{2,18},{18,2},{3,19},{19,3},{4,20},{20... | collective-permute-start | bytes 12582920 | tf_op jit(solution)/shard_map/ppermute | solution.py:29
  204.5 21.0 %collective-permute-start.19 = (bf16[1,1024]{1,0:T(2,128)(2,1)S(1)}, bf16[1,1024]{1,0:T(2,128)(2,1)S(1)}, u32[]{:S(2)}, u32[]{:S(2)}) collective-permute-start(bf16[1,1024]{1,0:T(2,128)(2,1)S(1)} %slice.450), channel_id=1, source_target_pairs={{0,1},{1,2},{2,3},{3,4},{4,5},{5,6},{6,7},{7,8},{8,9},{9,10},{10,1... | collective-permute-start | bytes 6152 | tf_op jit(solution)/shard_map/ppermute | solution.py:550
  238.4 27.3 %collective-permute-start.40 = (bf16[16,128,1024]{2,1,0:T(8,128)(2,1)}, bf16[16,128,1024]{2,1,0:T(8,128)(2,1)}, u32[]{:S(2)}, u32[]{:S(2)}) collective-permute-start(bf16[16,128,1024]{2,1,0:T(8,128)(2,1)} %bitcast.30), channel_id=1, source_target_pairs={{0,16},{16,0},{1,17},{17,1},{2,18},{18,2},{3,19},{19,3},{4,20},{20... | collective-permute-start | bytes 12582920 | tf_op jit(solution)/shard_map/ppermute | solution.py:29
  279.1 49.6 %collective-permute-start.47 = (bf16[16,160,1024]{2,1,0:T(8,128)(2,1)}, bf16[16,160,1024]{2,1,0:T(8,128)(2,1)}, u32[]{:S(2)}, u32[]{:S(2)}) collective-permute-start(bf16[16,160,1024]{2,1,0:T(8,128)(2,1)} %pad_maximum_fusion.1), channel_id=1, source_target_pairs={{0,16},{16,0},{1,17},{17,1},{2,18},{18,2},{3,19},{19,3},{4,20},{20... | collective-permute-start | bytes 15728648 | tf_op jit(solution)/shard_map/ppermute | solution.py:29
  286.4 7.7 %collective-permute-start.41 = (bf16[1,128,1024]{2,1,0:T(8,128)(2,1)}, bf16[1,128,1024]{2,1,0:T(8,128)(2,1)S(1)}, u32[]{:S(2)}, u32[]{:S(2)}) collective-permute-start(bf16[1,128,1024]{2,1,0:T(8,128)(2,1)} %get-tuple-element.217), channel_id=1, source_target_pairs={{0,1},{1,0},{2,3},{3,2},{4,5},{5,4},{6,7},{7,6},{8,9},{9,8},{10,11... | collective-permute-start | bytes 786440 | tf_op jit(solution)/shard_map/ppermute | solution.py:24
  287.8 7.4 %collective-permute-start.42 = (bf16[1,128,1024]{2,1,0:T(8,128)(2,1)}, bf16[1,128,1024]{2,1,0:T(8,128)(2,1)}, u32[]{:S(2)}, u32[]{:S(2)}) collective-permute-start(bf16[1,128,1024]{2,1,0:T(8,128)(2,1)} %get-tuple-element.216), channel_id=1, source_target_pairs={{0,2},{1,3},{2,0},{3,1},{4,6},{5,7},{6,4},{7,5},{8,10},{9,11},{10,... | collective-permute-start | bytes 786440 | tf_op jit(solution)/shard_map/ppermute | solution.py:24
  289.7 18.0 %collective-permute-start.44 = (bf16[2,128,1024]{2,1,0:T(8,128)(2,1)S(1)}, bf16[2,128,1024]{2,1,0:T(8,128)(2,1)S(1)}, u32[]{:S(2)}, u32[]{:S(2)}) collective-permute-start(bf16[2,128,1024]{2,1,0:T(8,128)(2,1)S(1)} %slice.464), channel_id=1, source_target_pairs={{0,1},{1,0},{2,3},{3,2},{4,5},{5,4},{6,7},{7,6},{8,9},{9,8},{10,11... | collective-permute-start | bytes 1572872 | tf_op jit(solution)/shard_map/ppermute | solution.py:24
  297.4 11.7 %collective-permute-start.45 = (bf16[2,128,1024]{2,1,0:T(8,128)(2,1)S(1)}, bf16[2,128,1024]{2,1,0:T(8,128)(2,1)S(1)}, u32[]{:S(2)}, u32[]{:S(2)}) collective-permute-start(bf16[2,128,1024]{2,1,0:T(8,128)(2,1)S(1)} %pad_maximum_fusion.9), channel_id=1, source_target_pairs={{0,2},{1,3},{2,0},{3,1},{4,6},{5,7},{6,4},{7,5},{8,10},{9,11},{10,... | collective-permute-start | bytes 1572872 | tf_op jit(solution)/shard_map/ppermute | solution.py:24
  298.3 11.0 %collective-permute-start.46 = (bf16[2,128,1024]{2,1,0:T(8,128)(2,1)S(1)}, bf16[2,128,1024]{2,1,0:T(8,128)(2,1)S(1)}, u32[]{:S(2)}, u32[]{:S(2)}) collective-permute-start(bf16[2,128,1024]{2,1,0:T(8,128)(2,1)S(1)} %pad_maximum_fusion.10), channel_id=1, source_target_pairs={{0,4},{1,5},{2,6},{3,7},{4,0},{5,1},{6,2},{7,3},{8,12},{9,13},{10,... | collective-permute-start | bytes 1572872 | tf_op jit(solution)/shard_map/ppermute | solution.py:24
  306.1 10.7 %collective-permute-start.43 = (f32[1,1024]{1,0:T(1,128)S(1)}, f32[1,1024]{1,0:T(1,128)S(1)}, u32[]{:S(2)}, u32[]{:S(2)}) collective-permute-start(f32[1,1024]{1,0:T(1,128)S(1)} %slice.463), channel_id=1, source_target_pairs={{1,0},{2,1},{3,2},{4,3},{5,4},{6,5},{7,6},{8,7},{9,8},{10,9},{11,1... | collective-permute-start | bytes 12296 | tf_op jit(solution)/shard_map/ppermute | solution.py:591
  312.0 10.3 %collective-permute-start.50 = (bf16[2,128,1024]{2,1,0:T(8,128)(2,1)}, bf16[2,128,1024]{2,1,0:T(8,128)(2,1)}, u32[]{:S(2)}, u32[]{:S(2)}) collective-permute-start(bf16[2,128,1024]{2,1,0:T(8,128)(2,1)} %get-tuple-element.213), channel_id=1, source_target_pairs={{0,1},{1,0},{2,3},{3,2},{4,5},{5,4},{6,7},{7,6},{8,9},{9,8},{10,11... | collective-permute-start | bytes 1572872 | tf_op jit(solution)/shard_map/ppermute | solution.py:24
  312.6 10.2 %collective-permute-start.51 = (bf16[2,128,1024]{2,1,0:T(8,128)(2,1)}, bf16[2,128,1024]{2,1,0:T(8,128)(2,1)}, u32[]{:S(2)}, u32[]{:S(2)}) collective-permute-start(bf16[2,128,1024]{2,1,0:T(8,128)(2,1)} %get-tuple-element.212), channel_id=1, source_target_pairs={{0,2},{1,3},{2,0},{3,1},{4,6},{5,7},{6,4},{7,5},{8,10},{9,11},{10,... | collective-permute-start | bytes 1572872 | tf_op jit(solution)/shard_map/ppermute | solution.py:24
  313.8 9.8 %collective-permute-start.52 = (bf16[2,128,1024]{2,1,0:T(8,128)(2,1)}, bf16[2,128,1024]{2,1,0:T(8,128)(2,1)}, u32[]{:S(2)}, u32[]{:S(2)}) collective-permute-start(bf16[2,128,1024]{2,1,0:T(8,128)(2,1)} %get-tuple-element.211), channel_id=1, source_target_pairs={{0,4},{1,5},{2,6},{3,7},{4,0},{5,1},{6,2},{7,3},{8,12},{9,13},{10,... | collective-permute-start | bytes 1572872 | tf_op jit(solution)/shard_map/ppermute | solution.py:24
  326.7 51.2 %collective-permute-start.60 = (bf16[1,128,1024]{2,1,0:T(8,128)(2,1)}, bf16[1,128,1024]{2,1,0:T(8,128)(2,1)S(1)}, u32[]{:S(2)}, u32[]{:S(2)}) collective-permute-start(bf16[1,128,1024]{2,1,0:T(8,128)(2,1)} %slice.488), channel_id=1, source_target_pairs={{0,8},{1,9},{2,10},{3,11},{4,12},{5,13},{6,14},{7,15},{8,0},{9,1},... | collective-permute-start | bytes 786440 | tf_op jit(solution)/shard_map/ppermute | solution.py:24
  341.0 7.7 %collective-permute-start.48 = (bf16[1,160,1024]{2,1,0:T(8,128)(2,1)S(1)}, bf16[1,160,1024]{2,1,0:T(8,128)(2,1)S(1)}, u32[]{:S(2)}, u32[]{:S(2)}) collective-permute-start(bf16[1,160,1024]{2,1,0:T(8,128)(2,1)S(1)} %get-tuple-element.199), channel_id=1, source_target_pairs={{0,1},{1,0},{2,3},{3,2},{4,5},{5,4},{6,7},{7,6},{8,9},{9,8},{10,11... | collective-permute-start | bytes 983048 | tf_op jit(solution)/shard_map/ppermute | solution.py:24
  343.4 34.5 %collective-permute-start.57 = (bf16[2,160,1024]{2,1,0:T(8,128)(2,1)S(1)}, bf16[2,160,1024]{2,1,0:T(8,128)(2,1)S(1)}, u32[]{:S(2)}, u32[]{:S(2)}) collective-permute-start(bf16[2,160,1024]{2,1,0:T(8,128)(2,1)S(1)} %slice.482), channel_id=1, source_target_pairs={{0,1},{1,0},{2,3},{3,2},{4,5},{5,4},{6,7},{7,6},{8,9},{9,8},{10,11... | collective-permute-start | bytes 1966088 | tf_op jit(solution)/shard_map/ppermute | solution.py:24
  352.3 7.9 %collective-permute-start.53 = (f32[1,2,1024]{2,1,0:T(2,128)S(1)}, f32[1,2,1024]{2,1,0:T(2,128)S(1)}, u32[]{:S(2)}, u32[]{:S(2)}) collective-permute-start(f32[1,2,1024]{2,1,0:T(2,128)S(1)} %bitcast.204), channel_id=1, source_target_pairs={{0,1},{1,0},{2,3},{3,2},{4,5},{5,4},{6,7},{7,6},{8,9},{9,8},{10,11... | collective-permute-start | bytes 24584 | tf_op jit(solution)/shard_map/ppermute | solution.py:24
  354.7 23.2 %collective-permute-start.58 = (bf16[2,160,1024]{2,1,0:T(8,128)(2,1)S(1)}, bf16[2,160,1024]{2,1,0:T(8,128)(2,1)S(1)}, u32[]{:S(2)}, u32[]{:S(2)}) collective-permute-start(bf16[2,160,1024]{2,1,0:T(8,128)(2,1)S(1)} %pad_maximum_fusion.3), channel_id=1, source_target_pairs={{0,2},{1,3},{2,0},{3,1},{4,6},{5,7},{6,4},{7,5},{8,10},{9,11},{10,... | collective-permute-start | bytes 1966088 | tf_op jit(solution)/shard_map/ppermute | solution.py:24
  355.1 22.9 %collective-permute-start.59 = (bf16[2,160,1024]{2,1,0:T(8,128)(2,1)S(1)}, bf16[2,160,1024]{2,1,0:T(8,128)(2,1)S(1)}, u32[]{:S(2)}, u32[]{:S(2)}) collective-permute-start(bf16[2,160,1024]{2,1,0:T(8,128)(2,1)S(1)} %pad_maximum_fusion.4), channel_id=1, source_target_pairs={{0,4},{1,5},{2,6},{3,7},{4,0},{5,1},{6,2},{7,3},{8,12},{9,13},{10,... | collective-permute-start | bytes 1966088 | tf_op jit(solution)/shard_map/ppermute | solution.py:24
  392.1 30.3 %collective-permute-start.70 = (bf16[16,128,1024]{2,1,0:T(8,128)(2,1)}, bf16[16,128,1024]{2,1,0:T(8,128)(2,1)}, u32[]{:S(2)}, u32[]{:S(2)}) collective-permute-start(bf16[16,128,1024]{2,1,0:T(8,128)(2,1)} %get-tuple-element.65), channel_id=1, source_target_pairs={{0,16},{16,0},{1,17},{17,1},{2,18},{18,2},{3,19},{19,3},{4,20},{20... | collective-permute-start | bytes 12582920 | tf_op jit(solution)/shard_map/ppermute | solution.py:29
  404.4 16.4 %collective-permute-start.61 = (bf16[2,160,1024]{2,1,0:T(8,128)(2,1)S(1)}, bf16[2,160,1024]{2,1,0:T(8,128)(2,1)S(1)}, u32[]{:S(2)}, u32[]{:S(2)}) collective-permute-start(bf16[2,160,1024]{2,1,0:T(8,128)(2,1)S(1)} %get-tuple-element.195), channel_id=1, source_target_pairs={{0,1},{1,0},{2,3},{3,2},{4,5},{5,4},{6,7},{7,6},{8,9},{9,8},{10,11... | collective-permute-start | bytes 1966088 | tf_op jit(solution)/shard_map/ppermute | solution.py:24
  405.3 16.0 %collective-permute-start.62 = (bf16[2,160,1024]{2,1,0:T(8,128)(2,1)S(1)}, bf16[2,160,1024]{2,1,0:T(8,128)(2,1)S(1)}, u32[]{:S(2)}, u32[]{:S(2)}) collective-permute-start(bf16[2,160,1024]{2,1,0:T(8,128)(2,1)S(1)} %get-tuple-element.194), channel_id=1, source_target_pairs={{0,2},{1,3},{2,0},{3,1},{4,6},{5,7},{6,4},{7,5},{8,10},{9,11},{10,... | collective-permute-start | bytes 1966088 | tf_op jit(solution)/shard_map/ppermute | solution.py:24
  406.7 15.7 %collective-permute-start.63 = (bf16[2,160,1024]{2,1,0:T(8,128)(2,1)S(1)}, bf16[2,160,1024]{2,1,0:T(8,128)(2,1)S(1)}, u32[]{:S(2)}, u32[]{:S(2)}) collective-permute-start(bf16[2,160,1024]{2,1,0:T(8,128)(2,1)S(1)} %get-tuple-element.193), channel_id=1, source_target_pairs={{0,4},{1,5},{2,6},{3,7},{4,0},{5,1},{6,2},{7,3},{8,12},{9,13},{10,... | collective-permute-start | bytes 1966088 | tf_op jit(solution)/shard_map/ppermute | solution.py:24
  407.8 30.0 %collective-permute-start.83 = (bf16[128,1024]{1,0:T(8,128)(2,1)S(1)}, bf16[128,1024]{1,0:T(8,128)(2,1)S(1)}, u32[]{:S(2)}, u32[]{:S(2)}) collective-permute-start(bf16[128,1024]{1,0:T(8,128)(2,1)S(1)} %fusion.43), channel_id=1, source_target_pairs={{0,16},{16,0},{1,17},{17,1},{2,18},{18,2},{3,19},{19,3},{4,20},{20... | collective-permute-start | bytes 786440 | tf_op jit(solution)/shard_map/ppermute | solution.py:29
  436.2 11.6 %collective-permute-start.72 = (bf16[2,128,1024]{2,1,0:T(8,128)(2,1)}, bf16[2,128,1024]{2,1,0:T(8,128)(2,1)}, u32[]{:S(2)}, u32[]{:S(2)}) collective-permute-start(bf16[2,128,1024]{2,1,0:T(8,128)(2,1)} %pad_maximum_fusion.11), channel_id=1, source_target_pairs={{0,4},{1,5},{2,6},{3,7},{4,0},{5,1},{6,2},{7,3},{8,12},{9,13},{10,... | collective-permute-start | bytes 1572872 | tf_op jit(solution)/shard_map/ppermute | solution.py:24
  437.3 11.2 %collective-permute-start.77 = (bf16[2,128,1024]{2,1,0:T(8,128)(2,1)}, bf16[2,128,1024]{2,1,0:T(8,128)(2,1)}, u32[]{:S(2)}, u32[]{:S(2)}) collective-permute-start(bf16[2,128,1024]{2,1,0:T(8,128)(2,1)} %pad_maximum_fusion.12), channel_id=1, source_target_pairs={{0,2},{1,3},{2,0},{3,1},{4,6},{5,7},{6,4},{7,5},{8,10},{9,11},{10,... | collective-permute-start | bytes 1572872 | tf_op jit(solution)/shard_map/ppermute | solution.py:24
  442.5 11.0 %collective-permute-start.66 = (f32[11,1024]{1,0:T(8,128)S(1)}, f32[11,1024]{1,0:T(8,128)S(1)}, u32[]{:S(2)}, u32[]{:S(2)}) collective-permute-start(f32[11,1024]{1,0:T(8,128)S(1)} %add.400), channel_id=1, source_target_pairs={{0,2},{1,3},{2,0},{3,1},{4,6},{5,7},{6,4},{7,5},{8,10},{9,11},{10,... | collective-permute-start | bytes 135176 | tf_op jit(solution)/shard_map/ppermute | solution.py:129
  450.3 24.2 %collective-permute-start.74 = (bf16[2,128,1024]{2,1,0:T(8,128)(2,1)S(1)}, bf16[2,128,1024]{2,1,0:T(8,128)(2,1)S(1)}, u32[]{:S(2)}, u32[]{:S(2)}) collective-permute-start(bf16[2,128,1024]{2,1,0:T(8,128)(2,1)S(1)} %get-tuple-element.204), channel_id=1, source_target_pairs={{0,1},{1,0},{2,3},{3,2},{4,5},{5,4},{6,7},{7,6},{8,9},{9,8},{10,11... | collective-permute-start | bytes 1572872 | tf_op jit(solution)/shard_map/ppermute | solution.py:24
  452.9 38.2 %collective-permute-start.81 = (bf16[1,160,1024]{2,1,0:T(8,128)(2,1)S(1)}, bf16[1,160,1024]{2,1,0:T(8,128)(2,1)S(1)}, u32[]{:S(2)}, u32[]{:S(2)}) collective-permute-start(bf16[1,160,1024]{2,1,0:T(8,128)(2,1)S(1)} %slice.527), channel_id=1, source_target_pairs={{0,8},{1,9},{2,10},{3,11},{4,12},{5,13},{6,14},{7,15},{8,0},{9,1},... | collective-permute-start | bytes 983048 | tf_op jit(solution)/shard_map/ppermute | solution.py:24
  458.3 13.8 %collective-permute-start.68 = (f32[11,1024]{1,0:T(8,128)S(1)}, f32[11,1024]{1,0:T(8,128)S(1)}, u32[]{:S(2)}, u32[]{:S(2)}) collective-permute-start(f32[11,1024]{1,0:T(8,128)S(1)} %add.402), channel_id=1, source_target_pairs={{0,8},{1,9},{2,10},{3,11},{4,12},{5,13},{6,14},{7,15},{8,0},{9,1},... | collective-permute-start | bytes 135176 | tf_op jit(solution)/shard_map/ppermute | solution.py:129
  473.9 13.5 %collective-permute-start.78 = (bf16[2,128,1024]{2,1,0:T(8,128)(2,1)S(1)}, bf16[2,128,1024]{2,1,0:T(8,128)(2,1)S(1)}, u32[]{:S(2)}, u32[]{:S(2)}) collective-permute-start(bf16[2,128,1024]{2,1,0:T(8,128)(2,1)S(1)} %get-tuple-element.203), channel_id=1, source_target_pairs={{0,4},{1,5},{2,6},{3,7},{4,0},{5,1},{6,2},{7,3},{8,12},{9,13},{10,... | collective-permute-start | bytes 1572872 | tf_op jit(solution)/shard_map/ppermute | solution.py:24
  473.9 13.5 %collective-permute-start.73 = (bf16[2,128,1024]{2,1,0:T(8,128)(2,1)S(1)}, bf16[2,128,1024]{2,1,0:T(8,128)(2,1)S(1)}, u32[]{:S(2)}, u32[]{:S(2)}) collective-permute-start(bf16[2,128,1024]{2,1,0:T(8,128)(2,1)S(1)} %get-tuple-element.202), channel_id=1, source_target_pairs={{0,1},{1,0},{2,3},{3,2},{4,5},{5,4},{6,7},{7,6},{8,9},{9,8},{10,11... | collective-permute-start | bytes 1572872 | tf_op jit(solution)/shard_map/ppermute | solution.py:24
  475.7 13.1 %collective-permute-start.75 = (bf16[2,128,1024]{2,1,0:T(8,128)(2,1)S(1)}, bf16[2,128,1024]{2,1,0:T(8,128)(2,1)S(1)}, u32[]{:S(2)}, u32[]{:S(2)}) collective-permute-start(bf16[2,128,1024]{2,1,0:T(8,128)(2,1)S(1)} %slice_add_fusion.5), channel_id=1, source_target_pairs={{0,2},{1,3},{2,0},{3,1},{4,6},{5,7},{6,4},{7,5},{8,10},{9,11},{10,... | collective-permute-start | bytes 1572872 | tf_op jit(solution)/shard_map/ppermute | solution.py:24
  490.0 13.8 %collective-permute-start.79 = (bf16[1,128,1024]{2,1,0:T(8,128)(2,1)S(1)}, bf16[1,128,1024]{2,1,0:T(8,128)(2,1)S(1)}, u32[]{:S(2)}, u32[]{:S(2)}) collective-permute-start(bf16[1,128,1024]{2,1,0:T(8,128)(2,1)S(1)} %slice.516), channel_id=1, source_target_pairs={{0,8},{1,9},{2,10},{3,11},{4,12},{5,13},{6,14},{7,15},{8,0},{9,1},... | collective-permute-start | bytes 786440 | tf_op jit(solution)/shard_map/ppermute | solution.py:24
  491.2 14.2 %collective-permute-start.82 = (bf16[160,1024]{1,0:T(8,128)(2,1)S(1)}, bf16[160,1024]{1,0:T(8,128)(2,1)S(1)}, u32[]{:S(2)}, u32[]{:S(2)}) collective-permute-start(bf16[160,1024]{1,0:T(8,128)(2,1)S(1)} %fusion.40), channel_id=1, source_target_pairs={{0,16},{16,0},{1,17},{17,1},{2,18},{18,2},{3,19},{19,3},{4,20},{20... | collective-permute-start | bytes 983048 | tf_op jit(solution)/shard_map/ppermute | solution.py:29
  (107 other events, 980.1 us)
